TPU v7x, 32 devices: a whole 2x2x4 slice. The times are simulated.
32 devices in a mesh: pb: 8 (over z, core), pa: 4 (over y, x).
Axes of the slice: x: 2, y: 2, z: 4, core: 2. Of those that a mesh axis runs over, the one named last changes fastest.
Arguments:
- queries: bfloat16 [2560, 768], P(('pb', 'pa')), may hold values from -8 to 8
- passages: bfloat16 [2560, 768], P(('pb', 'pa')), may hold values from -8 to 8
- positives: int32 [2560], P('pb'), may hold values from 0 to 2559, each once
- inv_temp: float32 [], replicated, may hold values from 80 to 320
Outputs:
- query_loss: float32 [2560], P(('pb', 'pa'))
- query_grads: bfloat16 [2560, 768], P(('pb', 'pa'))
- passage_grads: bfloat16 [2560, 768], P(('pb', 'pa'))
Inputs may be any that keep to these rules, and one draw needn't show every extreme that they name: `positives`: each passage is the positive of exactly one query.
All inputs are finite; a program needn't handle non-finite values.
Results may differ from a plain program's by a relative error of at most 0.02.
Values may be sent and summed in bfloat16 or wider, within the bound.
A program may use at most 64 MiB of HBM per device.

v0:
```python
import math

import jax
import jax.numpy as jnp
from jax import lax
from jax.sharding import PartitionSpec as P


def unit_rows(values):
    wide = values.astype(jnp.float32)
    length = jnp.sqrt(jnp.sum(wide * wide, axis=1, keepdims=True))
    return (wide / length, length)


def unit_back(unit, length, grad):
    along = jnp.sum(unit * grad, axis=1, keepdims=True)
    return ((grad - unit * along) / length).astype(jnp.bfloat16)


def similar(rows, column_rows, inv_temp):
    product = lax.dot_general(
        rows, column_rows, (((1,), (1,)), ((), ())), preferred_element_type=jnp.float32
    )
    return product * inv_temp


def make_delta(rows, totals, targets, column_rows, inv_temp):
    logits = similar(rows, column_rows, inv_temp)
    cols = lax.broadcasted_iota(jnp.int32, logits.shape, 1)
    hit = cols == targets[:, None]
    return (jnp.exp(logits - totals[:, None]) - jnp.where(hit, 1.0, 0.0)).astype(jnp.bfloat16)


def local(queries, passages, positives, inv_temp):
    tok_rows = queries.shape[0]
    width = queries.shape[1]
    query_unit, query_len = unit_rows(queries)
    passage_unit, passage_len = unit_rows(passages)
    query_low = query_unit.astype(jnp.bfloat16)
    passage_low = passage_unit.astype(jnp.bfloat16)
    query_block = lax.all_gather(query_low, "pa", axis=0, tiled=True)
    passage_block = lax.all_gather(passage_low, "pb", axis=0, tiled=True)
    row_count = query_block.shape[0]
    here = lax.axis_index("pa")
    span = lax.axis_size("pa")
    shard = positives // tok_rows
    owner = shard % span
    target = jnp.where(owner == here, shard // span * tok_rows + positives % tok_rows, -1)
    block = math.gcd(row_count, 1024)
    count_blocks = row_count // block
    query_tiles = query_block.reshape(count_blocks, block, width)
    target_tiles = target.reshape(count_blocks, block)

    def block_stats(inputs):
        rows, targets = inputs
        logits = similar(rows, passage_block, inv_temp)
        biggest = jnp.max(logits, axis=1)
        expsum = jnp.sum(jnp.exp(logits - biggest[:, None]), axis=1)
        cols = lax.broadcasted_iota(jnp.int32, logits.shape, 1)
        positive = jnp.sum(jnp.where(cols == targets[:, None], logits, 0.0), axis=1)
        return (biggest, expsum, positive)

    biggest, expsum, positive = lax.map(block_stats, (query_tiles, target_tiles))
    biggest = biggest.reshape(row_count)
    expsum = expsum.reshape(row_count)
    positive = positive.reshape(row_count)
    top = lax.pmax(biggest, "pa")
    summed, positive_all = lax.psum((expsum * jnp.exp(biggest - top), positive), "pa")
    totals = top + jnp.log(summed)
    losses = totals - positive_all
    query_loss = lax.dynamic_slice_in_dim(losses, here * tok_rows, tok_rows, 0)
    col_count = passage_block.shape[0]

    def tile_delta(inputs):
        rows, part_totals, part_targets = inputs
        return make_delta(rows, part_totals, part_targets, passage_block, inv_temp)

    stored = lax.map(tile_delta, (query_tiles, totals.reshape(count_blocks, block), target_tiles))
    stored = stored.reshape(row_count, col_count)
    delta = stored
    unit_qgrad = lax.psum_scatter(
        (inv_temp * jnp.dot(delta, passage_block, preferred_element_type=jnp.float32)).astype(
            jnp.bfloat16
        ),
        "pa",
        scatter_dimension=0,
        tiled=True,
    ).astype(jnp.float32)
    delta = stored
    update = lax.dot_general(
        delta, query_block, (((0,), (0,)), ((), ())), preferred_element_type=jnp.float32
    )
    unit_pgrad = lax.psum_scatter(
        (inv_temp * update).astype(jnp.bfloat16), "pb", scatter_dimension=0, tiled=True
    ).astype(jnp.float32)
    query_grads = unit_back(query_unit, query_len, unit_qgrad)
    passage_grads = unit_back(passage_unit, passage_len, unit_pgrad)
    return (query_loss, query_grads, passage_grads)


def solution(mesh):
    return jax.shard_map(
        local,
        mesh=mesh,
        in_specs=(P(("pb", "pa"), None), P(("pb", "pa"), None), P("pb"), P()),
        out_specs=(P(("pb", "pa")), P(("pb", "pa"), None), P(("pb", "pa"), None)),
        check_vma=False,
    )
```

profile of v0, /device:TPU:0, one launch (start us, length us, event | category | flops | bytes accessed | tf_op | source)
XLA Modules:
  0.0 142.4 jit_solution(10204770685166482322)
XLA Ops:
  7.9 1.0 fusion.15
  8.9 1.0 fusion.16
  10.0 0.7 fusion.26
  10.8 1.0 fusion.31
  11.8 1.0 fusion.30
  12.8 11.4 %all_gather.6 = bf16[320,768]{1,0:T(8,128)(2,1)S(1)} all-gather(bf16[80,768]{1,0:T(8,128)(2,1)S(1)} %fusion.30), channel_id=1, replica_groups=mesh['pb'=8,'pa'=4] {'pa'}, dimensions={0}, use_global_device_ids=true | all-gather | bytes 614400 | tf_op jit(solution)/shard_map/all_gather | solution.py:41
  24.2 17.1 %all_gather.7 = bf16[640,768]{1,0:T(8,128)(2,1)S(1)} all-gather(bf16[80,768]{1,0:T(8,128)(2,1)S(1)} %fusion.31), channel_id=1, replica_groups=mesh['pb'=8,'pa'=4] {'pb'}, dimensions={0}, use_global_device_ids=true | all-gather | bytes 1105920 | tf_op jit(solution)/shard_map/all_gather | solution.py:42
  41.3 7.7 %while.24 = (s32[]{:T(128)}, f32[5,64]{1,0:T(8,128)S(1)}, f32[5,64]{1,0:T(8,128)S(1)}, f32[5,64]{1,0:T(8,128)S(1)}, bf16[5,64,768]{2,1,0:T(8,128)(2,1)S(1)}, /*i...) while((s32[]{:T(128)}, f32[5,64]{1,0:T(8,128)S(1)}, ...), condition=%wide.region_6.7_spmd, body=%wide.region_2.6_spmd.sunk | while | flops 63201088 | bytes 1412485 | solution.py:63
  41.3 1.2 fusion.48
  42.5 0.2 select_reduce_fusion.2
  42.8 1.2 fusion.48
  44.0 0.2 select_reduce_fusion.2
  44.3 1.2 fusion.48
  45.9 1.2 fusion.48
  47.4 1.2 fusion.48
  49.1 8.9 %pmax.7 = f32[320]{0:T(512)S(1)} all-reduce(f32[320]{0:T(512)S(1)} %reshape.46), channel_id=1, replica_groups=mesh['pb'=8,'pa'=4] {'pa'}, use_global_device_ids=true, to_apply=%region_7.8 | all-reduce | flops 320 | bytes 2560 | tf_op jit(solution)/shard_map/pmax | solution.py:67
  58.1 8.9 %all-reduce = (f32[320]{0:T(512)S(1)}, f32[320]{0:T(512)S(1)}) all-reduce(f32[320]{0:T(512)S(1)} %exponential_multiply_fusion, f32[320]{0:T(512)S(1)} %reshape.48), channel_id=1, replica_groups=mesh['pb'=8,'pa'=4] {'pa'}, use_global_device_ids=true, to_apply=%region_8.9 | all-reduce | flops 640 | bytes 5120 | tf_op jit(solution)/shard_map/psum | solution.py:68
  67.0 5.7 %while.25 = (s32[]{:T(128)}, bf16[5,64,640]{2,1,0:T(8,128)(2,1)S(1)}, bf16[5,64,768]{2,1,0:T(8,128)(2,1)S(1)}, bf16[640,768]{1,0:T(8,128)(2,1)S(1)}, f32[]{:T(12...) while((s32[]{:T(128)}, bf16[5,64,640]{2,1,0:T(8,128)(2,1)S(1)}, ...), condition=%wide.region_11.12_spmd, body=%wide.region_10.11_spmd.sunk | while | flops 63160320 | bytes 1166441 | solution.py:78
  67.1 1.1 fusion.53
  68.2 1.1 fusion.53
  69.4 1.1 fusion.53
  70.5 1.1 fusion.53
  71.7 1.1 fusion.53
  72.8 1.3 fusion.14
  74.2 1.7 %multiply_convert_fusion = bf16[640,768]{1,0:T(8,128)(2,1)} fusion(bf16[320,640]{1,0:T(8,128)(2,1)S(1)} %bitcast.57, bf16[320,768]{1,0:T(8,128)(2,1)S(1)} %bitcast.52, f32[]{:T(128)S(6)} %copy.29), kind=kOutput, calls=%fused_computation.23 | convolution fusion | flops 315555840 | bytes 1884164 | tf_op jit(solution)/shard_map/dot_general | solution.py:90
  75.9 0.6 dynamic_slice.21
  76.5 22.0 %reduce-scatter.3.cloned.1.call-done = bf16[80,768]{1,0:T(8,128)(2,1)} async-done(((bf16[320,768]{1,0:T(8,128)(2,1)}), bf16[80,768]{1,0:T(8,128)(2,1)}) %reduce-scatter.3.cloned.1.call-update) | async-done | bytes 122896 | tf_op jit(solution)/shard_map/reduce_scatter | solution.py:81
  98.5 1.1 fusion.17
  99.6 1.7 %fusion.19 = bf16[80,768]{1,0:T(8,128)(2,1)} fusion(bf16[80,768]{1,0:T(8,128)(2,1)} %reduce-scatter.3.cloned.1.call-done, f32[80]{0:T(128)S(1)} %fusion.17, f32[80]{0:T(128)S(1)} %sqrt.16, bf16[80,768]{1,0:T(8,128)(2,1)S(1)} %copy-done), kind=kLoop, calls=%fused_computation.38 | loop fusion | flops 430080 | bytes 369280 | tf_op jit(solution)/shard_map/convert_element_type | solution.py:17
  101.3 31.5 %reduce-scatter.5.cloned.1.call-done = bf16[80,768]{1,0:T(8,128)(2,1)} async-done(((bf16[640,768]{1,0:T(8,128)(2,1)}), bf16[80,768]{1,0:T(8,128)(2,1)}) %reduce-scatter.5.cloned.1.call-update) | async-done | bytes 122896 | tf_op jit(solution)/shard_map/reduce_scatter | solution.py:93
  132.8 1.1 fusion.20
  133.9 1.7 %fusion.22 = bf16[80,768]{1,0:T(8,128)(2,1)} fusion(bf16[80,768]{1,0:T(8,128)(2,1)} %reduce-scatter.5.cloned.1.call-done, f32[80]{0:T(128)S(1)} %fusion.20, f32[80]{0:T(128)S(1)} %sqrt.17, bf16[80,768]{1,0:T(8,128)(2,1)S(1)} %copy-done.1), kind=kLoop, calls=%fused_computation.41 | loop fusion | flops 430080 | bytes 369280 | tf_op jit(solution)/shard_map/convert_element_type | solution.py:17
  (54 shorter events, 1.9 us)
Async XLA Ops:
  7.2 91.4 %reduce-scatter.3.cloned.1.call-start = ((), (), s32[]{:S(2)}) async-start(), calls=%async_computation.2 | async-start | bytes 614400 | tf_op jit(solution)/shard_map/reduce_scatter | solution.py:81
  74.1 58.6 %reduce-scatter.5.cloned.1.call-start = ((), (), s32[]{:S(2)}) async-start(), calls=%async_computation.3 | async-start | bytes 1105920 | tf_op jit(solution)/shard_map/reduce_scatter | solution.py:93
  75.9 22.7 %copy-start = (bf16[80,768]{1,0:T(8,128)(2,1)S(1)}, bf16[80,768]{1,0:T(8,128)(2,1)}, u32[]{:S(2)}) copy-start(bf16[80,768]{1,0:T(8,128)(2,1)} %param.8) | copy-start | bytes 368644
  75.9 56.9 %copy-start.1 = (bf16[80,768]{1,0:T(8,128)(2,1)S(1)}, bf16[80,768]{1,0:T(8,128)(2,1)}, u32[]{:S(2)}) copy-start(bf16[80,768]{1,0:T(8,128)(2,1)} %param.9) | copy-start | bytes 368644
Sparse Core Ops, SparseCore 0:
  74.3 24.2 reduce-scatter.2
  100.9 31.8 reduce-scatter.4
where the time goes:
time: 143 us; the launch traced here: 142 us
  waiting for transfers between devices  53.5 us (37%)
  blocking collectives  46.3 us (32%)
  between operations  14.8 us (10%)
  matrix products  14.4 us (10%)
  other arithmetic  11.5 us (8%)
  local copies, waits for them, and re-layouts  1.65 us (1%)
    reduce_scatter x1, waiting for transfers between devices, local(): lax.psum_scatter((inv_temp * update).astype(jnp.bfloat16), 'pb', scatter_...  31.5 us
    reduce_scatter x1, waiting for transfers between devices, local(): lax.psum_scatter((inv_temp * jnp.dot(delta, passage_block, preferred_elem...  22 us
    all_gather x1, blocking collectives, local(): passage_block = lax.all_gather(passage_low, 'pb', axis=0, tiled=True)  17.1 us
    all_gather x1, blocking collectives, local(): query_block = lax.all_gather(query_low, 'pa', axis=0, tiled=True)  11.4 us
    dot_general x10, matrix products, similar(): lax.dot_general(rows, column_rows, (((1,), (1,)), ((), ())), preferred_el...  11.4 us
    pmax x1, blocking collectives, local(): top = lax.pmax(biggest, 'pa')  8.93 us
    psum x1, blocking collectives, local(): lax.psum((expsum * jnp.exp(biggest - top), positive), 'pa')  8.86 us
    convert_element_type x2, other arithmetic, unit_back(): return ((grad - unit * along) / length).astype(jnp.bfloat16)  3.38 us
  transfers between devices with their start and end apart: 2, of which 2 were waited for; matrix products, arithmetic and copies ran while one was open for 4% of the time, Pallas kernels for 0%

commit v1 on v0

v1 whole, which is shorter than its diff:
```python
import functools

import jax
import jax.numpy as jnp
from jax import lax
from jax.experimental import pallas as pl
from jax.experimental.pallas import tpu as pltpu
from jax.sharding import PartitionSpec as P

MESH = pl.DeviceIdType.MESH
F32 = jnp.float32
BF16 = jnp.bfloat16
LANES = 128
COLS = 8


def unit_rows(values):
    wide = values.astype(F32)
    length = jnp.sqrt(jnp.sum(wide * wide, axis=1, keepdims=True))
    return (wide / length, length)


def unit_back(unit, length, grad):
    along = jnp.sum(unit * grad, axis=1, keepdims=True)
    return ((grad - unit * along) / length).astype(BF16)


def repeat(count, body):
    if count <= 4:
        for k in range(count):
            body(k)
    else:

        @pl.loop(0, count)
        def _(k):
            body(k)


def kernel(
    na,
    nb,
    temp_ref,
    tgt_ref,
    q_ref,
    p_ref,
    loss_ref,
    qg_ref,
    pg_ref,
    qbuf,
    pbuf,
    tbuf,
    ebuf,
    dbuf,
    stat,
    pacc,
    psib_out,
    psib_in,
    px_out,
    px_in,
    pz_out,
    pz_in,
    qpart,
    qy_in,
    qz_out,
    qz_in,
    ps_send,
    ps_recv,
    qs_send,
    qs_recv,
    ts_send,
    ts_recv,
    ss_send,
    ss_recv,
    gp_send,
    gp_recv,
    gy_send,
    gy_recv,
    gz_send,
    gz_recv,
):
    rows = q_ref.shape[0]
    width = q_ref.shape[1]
    nr = na * nb
    pb = lax.axis_index("pb")
    pa = lax.axis_index("pa")
    zh, zl, co = pb // 4, (pb // 2) % 2, pb % 2
    yy, xx = pa // 2, pa % 2

    def dev(zh, zl, co, yy, xx):
        return (zh * 4 + zl * 2 + co, yy * 2 + xx)

    def wrap(v, n):
        return lax.rem(v, n)

    sib = dev(zh, zl, 1 - co, yy, xx)
    xnb = dev(zh, zl, co, yy, 1 - xx)
    znb = dev(zh, 1 - zl, co, yy, xx)

    def peer(dz, dy):
        return dev(wrap(zh + dz, na), zl, co, wrap(yy + dy, nb), xx)

    peers = [(dz, dy) for dz in range(na) for dy in range(nb) if dz or dy]

    barrier = pltpu.get_barrier_semaphore()
    for other in [sib, xnb, znb] + [peer(dz, dy) for dz, dy in peers]:
        pl.semaphore_signal(barrier, inc=1, device_id=other, device_id_type=MESH)

    def pslot(co, zl, xx):
        return pbuf.at[pl.ds(pl.multiple_of((co * 4 + zl * 2 + xx) * rows, 16), rows)]

    def qslot(dz, dy):
        i = wrap(zh + dz, na) * nb + wrap(yy + dy, nb)
        return qbuf.at[pl.ds(pl.multiple_of(i * LANES, LANES), rows)]

    def tslot(dz, dy):
        i = wrap(zh + dz, na) * nb + wrap(yy + dy, nb)
        return tbuf.at[i]

    def move(src, dst, send, recv, to):
        return pltpu.make_async_remote_copy(
            src_ref=src,
            dst_ref=dst,
            send_sem=send,
            recv_sem=recv,
            device_id=to,
            device_id_type=MESH,
        )

    sent = []

    def start(src, dst, send, recv, to):
        copy = move(src, dst, send, recv, to)
        copy.start()
        sent.append(copy)

    def arrive(dst, send, recv):
        move(dst, dst, send, recv, sib).wait_recv()

    p_unit, _ = unit_rows(p_ref[...])
    pslot(co, zl, xx)[...] = p_unit.astype(BF16)
    q_unit, _ = unit_rows(q_ref[...])
    qslot(0, 0)[...] = q_unit.astype(BF16)
    tslot(0, 0)[...] = tgt_ref[...]

    def clear(i):
        base = i * LANES + rows
        qbuf[pl.ds(pl.multiple_of(base, 16), LANES - rows), :] = jnp.zeros(
            (LANES - rows, width), BF16
        )

    repeat(nr, clear)
    pl.semaphore_wait(barrier, 3 + len(peers))

    def send_p(k, slot, to):
        start(slot, slot, ps_send.at[k], ps_recv.at[k], to)

    def take_p(k, slot):
        arrive(slot, ps_send.at[k], ps_recv.at[k])

    def qindex(dz, dy):
        return dz * nb + dy

    own = pslot(co, zl, xx)
    send_p(0, own, znb)
    send_p(1, own, xnb)
    mine = qslot(0, 0)
    for dz in range(1, na):
        k = qindex(dz, 0)
        start(mine, mine, qs_send.at[k], qs_recv.at[k], peer(dz, 0))
    for dy in range(1, nb):
        k = qindex(0, dy)
        start(mine, mine, qs_send.at[k], qs_recv.at[k], peer(0, dy))
    send_p(2, own, sib)
    for dz, dy in peers:
        k = qindex(dz, dy)
        start(tslot(0, 0), tslot(0, 0), ts_send.at[k], ts_recv.at[k], peer(dz, dy))

    from_z = pslot(co, 1 - zl, xx)
    take_p(0, from_z)
    send_p(3, from_z, xnb)
    send_p(4, from_z, sib)
    for dz in range(1, na):
        k = qindex(dz, 0)
        came = qslot(na - dz, 0)
        arrive(came, qs_send.at[k], qs_recv.at[k])
        for dy in range(1, nb):
            k = qindex(dz, dy)
            start(came, came, qs_send.at[k], qs_recv.at[k], peer(0, dy))
    from_x = pslot(co, zl, 1 - xx)
    take_p(1, from_x)
    send_p(5, from_x, sib)
    from_d = pslot(co, 1 - zl, 1 - xx)
    take_p(3, from_d)
    send_p(6, from_d, sib)
    for dz in range(na):
        for dy in range(1, nb):
            k = qindex(dz, dy)
            arrive(qslot((na - dz) % na, nb - dy), qs_send.at[k], qs_recv.at[k])
    for dz, dy in peers:
        k = qindex(dz, dy)
        arrive(tslot((na - dz) % na, (nb - dy) % nb), ts_send.at[k], ts_recv.at[k])
    take_p(2, pslot(1 - co, zl, xx))
    take_p(4, pslot(1 - co, 1 - zl, xx))
    take_p(5, pslot(1 - co, zl, 1 - xx))
    take_p(6, pslot(1 - co, 1 - zl, 1 - xx))

    inv_temp = temp_ref[0, 0]
    count = COLS * rows
    me_r = zh * nb + yy
    base = me_r * count
    my_stat = stat.at[me_r]

    def span(i):
        if isinstance(i, int):
            return pl.ds(i * LANES, LANES)
        return pl.ds(pl.multiple_of(i * LANES, LANES), LANES)

    def hits(i):
        target = tbuf[i][0:1, :] - base
        return lax.broadcasted_iota(jnp.int32, (count, LANES), 0) == target

    def forward(i):
        logits = (
            lax.dot_general(
                pbuf[...], qbuf[span(i), :], (((1,), (1,)), ((), ())), preferred_element_type=F32
            )
            * inv_temp
        )
        biggest = jnp.max(logits, axis=0, keepdims=True)
        powers = jnp.exp(logits - biggest)
        ebuf[:, span(i)] = powers
        my_stat[0:1, span(i)] = biggest
        my_stat[1:2, span(i)] = jnp.sum(powers, axis=0, keepdims=True)
        my_stat[2:3, span(i)] = jnp.sum(jnp.where(hits(i), logits, 0.0), axis=0, keepdims=True)

    repeat(nr, forward)

    for dz, dy in peers:
        k = qindex(dz, dy)
        start(my_stat, my_stat, ss_send.at[k], ss_recv.at[k], peer(dz, dy))
    for dz, dy in peers:
        k = qindex(dz, dy)
        i = wrap(zh + na - dz, na) * nb + wrap(yy + nb - dy, nb)
        arrive(stat.at[i], ss_send.at[k], ss_recv.at[k])

    top = stat[0, 0:1, :]
    for i in range(1, nr):
        top = jnp.maximum(top, stat[i, 0:1, :])
    summed = jnp.zeros_like(top)
    positive = jnp.zeros_like(top)
    for i in range(nr):
        summed += stat[i, 1:2, :] * jnp.exp(stat[i, 0:1, :] - top)
        positive += stat[i, 2:3, :]
    totals = top + jnp.log(summed)
    losses = totals - positive
    scale = jnp.exp(my_stat[0:1, :] - totals)
    picked = jnp.zeros((1, LANES), F32)
    for i in range(nr):
        picked = jnp.where(me_r == i, losses[:, i * LANES : (i + 1) * LANES], picked)
    loss_ref[...] = picked[:, :rows]
    stat[nr, 0:1, :] = scale

    def make_delta(i):
        part = ebuf[:, span(i)] * stat[nr, 0:1, span(i)]
        dbuf[:, span(i)] = (part - jnp.where(hits(i), 1.0, 0.0)).astype(BF16)

    repeat(nr, make_delta)

    half = count // 2

    def update(core):
        return (
            jnp.dot(
                dbuf[pl.ds(pl.multiple_of(core * half, 16), half), :],
                qbuf[...],
                preferred_element_type=F32,
            )
            * inv_temp
        )

    psib_out[...] = update(1 - co).astype(BF16)
    start(psib_out, psib_in, gp_send.at[0], gp_recv.at[0], sib)
    pacc[...] = update(co)
    arrive(psib_in, gp_send.at[0], gp_recv.at[0])

    def piece(zl, xx):
        at = pl.ds(pl.multiple_of((zl * 2 + xx) * rows, 16), rows)
        return pacc[at, :] + psib_in[at, :].astype(F32)

    px_out[0] = piece(1 - zl, 1 - xx).astype(BF16)
    start(px_out.at[0], px_in.at[0], gp_send.at[1], gp_recv.at[1], xnb)
    px_out[1] = piece(zl, 1 - xx).astype(BF16)
    start(px_out.at[1], px_in.at[1], gp_send.at[2], gp_recv.at[2], xnb)

    def query_part(i):
        part = lax.dot_general(
            dbuf[:, span(i)], pbuf[...], (((0,), (0,)), ((), ())), preferred_element_type=F32
        )
        qpart[i] = (part * inv_temp)[:rows].astype(BF16)

    repeat(nr, query_part)

    def part_at(dz, dy):
        return qpart.at[wrap(zh + dz, na) * nb + wrap(yy + dy, nb)]

    for dz in [*range(1, na), 0]:
        for dy in range(1, nb):
            k = qindex(dz, dy)
            start(part_at(dz, dy), qy_in.at[k], gy_send.at[k], gy_recv.at[k], peer(0, dy))

    arrive(px_in.at[0], gp_send.at[1], gp_recv.at[1])
    pz_out[...] = (piece(1 - zl, xx) + px_in[0].astype(F32)).astype(BF16)
    start(pz_out, pz_in, gp_send.at[3], gp_recv.at[3], znb)

    def gather_y(dz):
        total = part_at(dz, 0)[...].astype(F32)
        for dy in range(1, nb):
            k = qindex(dz, dy)
            arrive(qy_in.at[k], gy_send.at[k], gy_recv.at[k])
            total += qy_in[k].astype(F32)
        return total

    for dz in range(1, na):
        qz_out[dz] = gather_y(dz).astype(BF16)
        start(qz_out.at[dz], qz_in.at[dz], gz_send.at[dz], gz_recv.at[dz], peer(dz, 0))

    arrive(px_in.at[1], gp_send.at[2], gp_recv.at[2])
    grad = piece(zl, xx) + px_in[1].astype(F32)
    arrive(pz_in, gp_send.at[3], gp_recv.at[3])
    grad += pz_in[...].astype(F32)
    p_unit, p_len = unit_rows(p_ref[...])
    pg_ref[...] = unit_back(p_unit, p_len, grad)

    grad = gather_y(0)
    for dz in range(1, na):
        arrive(qz_in.at[dz], gz_send.at[dz], gz_recv.at[dz])
        grad += qz_in[dz].astype(F32)
    q_unit, q_len = unit_rows(q_ref[...])
    qg_ref[...] = unit_back(q_unit, q_len, grad)

    for copy in sent:
        copy.wait_send()


def local(na, nb, queries, passages, positives, inv_temp):
    rows, width = queries.shape
    nr = na * nb
    lanes = nr * LANES
    pa = lax.axis_index("pa")
    own = lax.dynamic_slice_in_dim(positives, pa * rows, rows, 0)
    shard = own // rows
    spb = shard // (nb * 2)
    spa = shard % (nb * 2)
    group = (spb // 4) * nb + spa // 2
    col = (spb % 2) * 4 + ((spb // 2) % 2) * 2 + spa % 2
    code = (group * COLS + col) * rows + own % rows
    code = jnp.pad(code.reshape(1, rows), ((0, 7), (0, LANES - rows)), constant_values=-1)
    block = (rows, width)
    vmem = pl.BlockSpec(memory_space=pltpu.VMEM)
    smem = pl.BlockSpec(memory_space=pltpu.SMEM)
    dma = pltpu.SemaphoreType.DMA
    loss, qg, pg = pl.pallas_call(
        functools.partial(kernel, na, nb),
        out_shape=(
            jax.ShapeDtypeStruct((1, rows), F32),
            jax.ShapeDtypeStruct(block, BF16),
            jax.ShapeDtypeStruct(block, BF16),
        ),
        in_specs=[smem, vmem, vmem, vmem],
        out_specs=(vmem, vmem, vmem),
        scratch_shapes=[
            pltpu.VMEM((lanes, width), BF16),
            pltpu.VMEM((COLS * rows, width), BF16),
            pltpu.VMEM((nr, 8, LANES), jnp.int32),
            pltpu.VMEM((COLS * rows, lanes), F32),
            pltpu.VMEM((COLS * rows, lanes), BF16),
            pltpu.VMEM((nr + 1, 8, lanes), F32),
            pltpu.VMEM((COLS * rows // 2, width), F32),
            pltpu.VMEM((COLS * rows // 2, width), BF16),
            pltpu.VMEM((COLS * rows // 2, width), BF16),
            pltpu.VMEM((2, *block), BF16),
            pltpu.VMEM((2, *block), BF16),
            pltpu.VMEM(block, BF16),
            pltpu.VMEM(block, BF16),
            pltpu.VMEM((nr, *block), BF16),
            pltpu.VMEM((nr, *block), BF16),
            pltpu.VMEM((na, *block), BF16),
            pltpu.VMEM((na, *block), BF16),
            dma((7,)),
            dma((7,)),
            dma((nr,)),
            dma((nr,)),
            dma((nr,)),
            dma((nr,)),
            dma((nr,)),
            dma((nr,)),
            dma((4,)),
            dma((4,)),
            dma((nr,)),
            dma((nr,)),
            dma((na,)),
            dma((na,)),
        ],
        compiler_params=pltpu.CompilerParams(
            collective_id=0, has_side_effects=True, vmem_limit_bytes=56 * 1024 * 1024
        ),
    )(inv_temp.reshape(1, 1), code, queries, passages)
    return (loss.reshape(rows), qg, pg)


def solution(mesh):
    na = mesh.shape["pb"] // 4
    nb = mesh.shape["pa"] // 2
    return jax.shard_map(
        functools.partial(local, na, nb),
        mesh=mesh,
        in_specs=(P(("pb", "pa"), None), P(("pb", "pa"), None), P("pb"), P()),
        out_specs=(P(("pb", "pa")), P(("pb", "pa"), None), P(("pb", "pa"), None)),
        check_vma=False,
    )
```

time: 143 us -> 46 us (0.32)
  waiting for transfers between devices: 53.5 us -> 0 us
  blocking collectives: 46.3 us -> 0 us
  Pallas kernels: 0 us -> 39.6 us
  matrix products: 14.4 us -> 0 us
  between operations: 14.8 us -> 1.3 us
  other arithmetic: 11.5 us -> 0.8 us
  local copies, waits for them, and re-layouts: 1.65 us -> 4.02 us
    reduce_scatter x2 -> x0, waiting for transfers between devices: 53.5 us -> none  [the longest x1 31.5 us: local(): lax.psum_scatter((inv_temp * update).astype(jnp.bfloat16), 'pb', scatter_...]
    pallas_call x0 -> x1, Pallas kernels: none -> 39.6 us  [local(): pl.pallas_call(functools.partial(kernel, na, nb), out_shape=(jax.ShapeDty...]
    all_gather x2 -> x0, blocking collectives: 28.5 us -> none  [the longest x1 17.1 us: local(): passage_block = lax.all_gather(passage_low, 'pb', axis=0, tiled=True)]
    dot_general x12 -> x0, matrix products: 14.4 us -> none  [the longest x10 11.4 us: similar(): lax.dot_general(rows, column_rows, (((1,), (1,)), ((), ())), preferred_el...]
    pmax x1 -> x0, blocking collectives: 8.93 us -> none  [local(): top = lax.pmax(biggest, 'pa')]
    psum x1 -> x0, blocking collectives: 8.86 us -> none  [local(): lax.psum((expsum * jnp.exp(biggest - top), positive), 'pa')]
    reduce_sum x9 -> x0, other arithmetic: 5.38 us -> none  [the longest x2 2.23 us: unit_back(): along = jnp.sum(unit * grad, axis=1, keepdims=True)]
    convert_element_type x4 -> x0, other arithmetic: 5.36 us -> none  [the longest x2 3.38 us: unit_back(): return ((grad - unit * along) / length).astype(jnp.bfloat16)]
  transfers between devices with their start and end apart: 2 -> 0, of which waited for: 2 -> 0; matrix products, arithmetic and copies ran while one was open for 4% -> 0% of each run, Pallas kernels for 0% -> 0%
where the time goes in v1:
time: 46 us; the launch traced here: 45.7 us
  Pallas kernels  39.6 us (86%)
  local copies, waits for them, and re-layouts  4.02 us (9%)
  between operations  1.3 us (3%)
  other arithmetic  0.8 us (2%)
    pallas_call x1, Pallas kernels, local(): pl.pallas_call(functools.partial(kernel, na, nb), out_shape=(jax.ShapeDty...  39.6 us
    unnamed x7, local copies, waits for them, and re-layouts  3.42 us

profile of v1, /device:TPU:0, one launch (start us, length us, event | category | flops | bytes accessed | tf_op | source)
XLA Modules:
  0.0 45.7 jit_solution(12456908840352342526)
XLA Ops:
  1.3 0.8 %fusion.7 = s32[1,80]{1,0:T(1,128)S(1)} fusion(s32[320]{0:T(512)} %param.6, s32[]{:T(128)S(6)} %select_n.43), kind=kLoop, calls=%fused_computation.30 | loop fusion | flops 8000 | bytes 644 | tf_op jit(solution)/shard_map/reshape | solution.py:357
  2.1 0.6 %pad.4.tgt_ref = s32[8,128]{1,0:T(8,128)} pad(s32[1,80]{1,0:T(1,128)S(1)} %fusion.7, s32[]{:T(128)} %constant.89.clone.1), padding=0_7x0_48 | pad | bytes 4420 | tf_op jit(solution)/shard_map/jit(_pad)/pad | solution.py:357
  2.7 39.6 %shard_map.67 = (f32[1,80]{1,0:T(1,128)}, bf16[80,768]{1,0:T(8,128)(2,1)}, bf16[80,768]{1,0:T(8,128)(2,1)}) custom-call(f32[1,1]{1,0:T(1,128)} %bitcast.4.temp_ref, s32[8,128]{1,0:T(8,128)} %pad.4.tgt_ref, bf16[80,768]{1,0:T(8,128)(2,1)} %q_ref.1, bf16[80,768]{1,0:T(8,128)(2,1)} %p_ref.1), custom_call_target="tpu_custom_call" | custom-call | tf_op jit(solution)/shard_map/pallas_call | solution.py:362
  42.3 0.0 copy-start.1
  42.3 0.7 %copy-done.1 = f32[1,80]{1,0:T(1,128)S(1)} copy-done((f32[1,80]{1,0:T(1,128)S(1)}, f32[1,80]{1,0:T(1,128)}, u32[]{:S(2)}) %copy-start.1) | copy-done | bytes 344
  43.0 0.5 %copy.11 = f32[80]{0:T(128)} copy(f32[80]{0:T(128)S(1)} %bitcast.5) | data formatting | bytes 640
  43.5 0.0 copy-start
  43.5 1.6 %copy.12 = bf16[80,768]{1,0:T(8,128)(2,1)} copy(bf16[80,768]{1,0:T(8,128)(2,1)} %get-tuple-element.13) | data formatting | bytes 245760
  45.1 0.0 copy-done
  45.1 0.6 %copy.13 = bf16[80,768]{1,0:T(8,128)(2,1)} copy(bf16[80,768]{1,0:T(8,128)(2,1)S(1)} %copy-done) | data formatting | bytes 245760
Async XLA Ops:
  42.3 0.7 %copy-start.1 = (f32[1,80]{1,0:T(1,128)S(1)}, f32[1,80]{1,0:T(1,128)}, u32[]{:S(2)}) copy-start(f32[1,80]{1,0:T(1,128)} %get-tuple-element.6) | copy-start | bytes 964
  43.5 1.6 %copy-start = (bf16[80,768]{1,0:T(8,128)(2,1)S(1)}, bf16[80,768]{1,0:T(8,128)(2,1)}, u32[]{:S(2)}) copy-start(bf16[80,768]{1,0:T(8,128)(2,1)} %get-tuple-element.14) | copy-start | bytes 368644

commit v2 on v1

v2 whole, which is shorter than its diff:
```python
import functools

import jax
import jax.numpy as jnp
from jax import lax
from jax.experimental import pallas as pl
from jax.experimental.pallas import tpu as pltpu
from jax.sharding import PartitionSpec as P

MESH = pl.DeviceIdType.MESH
F32 = jnp.float32
BF16 = jnp.bfloat16
LANES = 128
COLS = 8
STEP = 16


def unit_rows(values):
    wide = values.astype(F32)
    length = jnp.sqrt(jnp.sum(wide * wide, axis=1, keepdims=True))
    return (wide / length, length)


def unit_back(unit, length, grad):
    along = jnp.sum(unit * grad, axis=1, keepdims=True)
    return ((grad - unit * along) / length).astype(BF16)


def repeat(count, body):
    if count <= 4:
        for k in range(count):
            body(k)
    else:

        @pl.loop(0, count)
        def _(k):
            body(k)


def kernel(
    na,
    nb,
    temp_ref,
    tgt_ref,
    q_hbm,
    p_hbm,
    loss_ref,
    qg_hbm,
    pg_hbm,
    q_ref,
    p_ref,
    qg_ref,
    pg_ref,
    qbuf,
    pbuf,
    tbuf,
    ebuf,
    dbuf,
    stat,
    pacc,
    psib_out,
    psib_in,
    px_out,
    px_in,
    pz_out,
    pz_in,
    qpart,
    qy_in,
    qz_out,
    qz_in,
    io_sem,
    ps_send,
    ps_recv,
    qs_send,
    qs_recv,
    ts_send,
    ts_recv,
    ss_send,
    ss_recv,
    gs_send,
    gs_recv,
    gp_send,
    gp_recv,
    gy_send,
    gy_recv,
    gz_send,
    gz_recv,
):
    rows = q_ref.shape[0]
    width = q_ref.shape[1]
    nr = na * nb
    steps = rows // STEP
    pb = lax.axis_index("pb")
    pa = lax.axis_index("pa")
    zh, zl, co = pb // 4, (pb // 2) % 2, pb % 2
    yy, xx = pa // 2, pa % 2

    def dev(zh, zl, co, yy, xx):
        return (zh * 4 + zl * 2 + co, yy * 2 + xx)

    def wrap(v, n):
        return lax.rem(v, n)

    sib = dev(zh, zl, 1 - co, yy, xx)
    xnb = dev(zh, zl, co, yy, 1 - xx)
    znb = dev(zh, 1 - zl, co, yy, xx)

    def peer(dz, dy):
        return dev(wrap(zh + dz, na), zl, co, wrap(yy + dy, nb), xx)

    peers = [(dz, dy) for dz in range(na) for dy in range(nb) if dz or dy]

    barrier = pltpu.get_barrier_semaphore()
    for other in [sib, xnb, znb] + [peer(dz, dy) for dz, dy in peers]:
        pl.semaphore_signal(barrier, inc=1, device_id=other, device_id_type=MESH)
    load_q = pltpu.make_async_copy(q_hbm, q_ref, io_sem.at[0])
    load_p = pltpu.make_async_copy(p_hbm, p_ref, io_sem.at[1])
    load_q.start()
    load_p.start()

    def member(dz, dy):
        return wrap(zh + dz, na) * nb + wrap(yy + dy, nb)

    def pslot(co, zl, xx, h=None):
        base = (co * 4 + zl * 2 + xx) * rows
        if h is None:
            return pbuf.at[pl.ds(pl.multiple_of(base, 16), rows)]
        return pbuf.at[pl.ds(pl.multiple_of(base + h * STEP, 16), STEP)]

    def qslot(dz, dy, h=None):
        base = member(dz, dy) * LANES
        if h is None:
            return qbuf.at[pl.ds(pl.multiple_of(base, LANES), rows)]
        return qbuf.at[pl.ds(pl.multiple_of(base + h * STEP, 16), STEP)]

    def tslot(dz, dy):
        return tbuf.at[member(dz, dy)]

    def move(src, dst, send, recv, to):
        return pltpu.make_async_remote_copy(
            src_ref=src,
            dst_ref=dst,
            send_sem=send,
            recv_sem=recv,
            device_id=to,
            device_id_type=MESH,
        )

    sent = []

    def start(src, dst, send, recv, to):
        copy = move(src, dst, send, recv, to)
        copy.start()
        sent.append(copy)

    def arrive(dst, send, recv):
        move(dst, dst, send, recv, sib).wait_recv()

    def clear(i):
        base = i * LANES + rows
        qbuf[pl.ds(pl.multiple_of(base, 16), LANES - rows), :] = jnp.zeros(
            (LANES - rows, width), BF16
        )

    repeat(nr, clear)

    positives = tgt_ref[...].reshape(1, -1)
    picked = jnp.zeros((1, rows), jnp.int32)
    for k in range(nb * 2):
        picked = jnp.where(pa == k, positives[:, k * rows : (k + 1) * rows], picked)
    me_r = member(0, 0)
    tbuf[me_r] = jnp.full((8, LANES), -1, jnp.int32)
    tbuf[me_r, 0:1, 0:rows] = picked

    load_q.wait()
    q_unit, _ = unit_rows(q_ref[...])
    qslot(0, 0)[...] = q_unit.astype(BF16)
    load_p.wait()
    p_unit, _ = unit_rows(p_ref[...])
    pslot(co, zl, xx)[...] = p_unit.astype(BF16)
    pl.semaphore_wait(barrier, 3 + len(peers))

    def send_p(k, co, zl, xx, to, h=None):
        slot = pslot(co, zl, xx, h)
        at = (k, h or 0)
        start(slot, slot, ps_send.at[at], ps_recv.at[at], to)

    def take_p(k, co, zl, xx, h=None):
        at = (k, h or 0)
        arrive(pslot(co, zl, xx, h), ps_send.at[at], ps_recv.at[at])

    def send_q(dz, dy, slot, to, h=None):
        at = (dz * nb + dy, h or 0)
        start(slot, slot, qs_send.at[at], qs_recv.at[at], to)

    def take_q(dz, dy, h=None):
        at = (dz * nb + dy, h or 0)
        slot = qslot((na - dz) % na, (nb - dy) % nb, h)
        arrive(slot, qs_send.at[at], qs_recv.at[at])

    for h in range(steps):
        for dz in range(1, na):
            send_q(dz, 0, qslot(0, 0, h), peer(dz, 0), h)
        send_p(0, co, zl, xx, znb, h)
    for dy in range(1, nb):
        send_q(0, dy, qslot(0, 0), peer(0, dy))
    send_p(1, co, zl, xx, xnb)
    send_p(2, co, zl, xx, sib)
    for dz, dy in peers:
        k = dz * nb + dy
        start(tslot(0, 0), tslot(0, 0), ts_send.at[k], ts_recv.at[k], peer(dz, dy))

    for h in range(steps):
        take_p(0, co, 1 - zl, xx, h)
        send_p(3, co, 1 - zl, xx, xnb, h)
        for dz in range(1, na):
            take_q(dz, 0, h)
            for dy in range(1, nb):
                send_q(dz, dy, qslot(na - dz, 0, h), peer(0, dy), h)
    send_p(4, co, 1 - zl, xx, sib)
    take_p(1, co, zl, 1 - xx)
    send_p(5, co, zl, 1 - xx, sib)
    for h in range(steps):
        take_p(3, co, 1 - zl, 1 - xx, h)
        send_p(6, co, 1 - zl, 1 - xx, sib, h)
    for dz, dy in peers:
        k = dz * nb + dy
        arrive(tslot((na - dz) % na, (nb - dy) % nb), ts_send.at[k], ts_recv.at[k])
    take_p(2, 1 - co, zl, xx)
    take_p(4, 1 - co, 1 - zl, xx)
    take_p(5, 1 - co, zl, 1 - xx)
    for h in range(steps):
        take_p(6, 1 - co, 1 - zl, 1 - xx, h)

    inv_temp = temp_ref[0, 0]
    count = COLS * rows
    my_stat = stat.at[me_r]
    down = lax.broadcasted_iota(jnp.int32, (rows, LANES), 0)
    ids = jnp.concatenate(
        [
            down + ((zh * 4 + (j // 2) % 2 * 2 + j // 4) * (nb * 2) + yy * 2 + j % 2) * rows
            for j in range(COLS)
        ],
        axis=0,
    )

    def span(i, n=1):
        if isinstance(i, int):
            return pl.ds(i * LANES, n * LANES)
        return pl.ds(pl.multiple_of(i * LANES, LANES), n * LANES)

    def hits(i):
        return ids == tbuf[i][0:1, :]

    def forward(i):
        both = (
            lax.dot_general(
                pbuf[...],
                qbuf[span(i, 2), :],
                (((1,), (1,)), ((), ())),
                preferred_element_type=F32,
            )
            * inv_temp
        )
        for k in range(2):
            logits = both[:, k * LANES : (k + 1) * LANES]
            biggest = jnp.max(logits, axis=0, keepdims=True)
            powers = jnp.exp(logits - biggest)
            at = span(i + k)
            ebuf[:, at] = powers
            my_stat[0:1, at] = biggest
            my_stat[1:2, at] = jnp.sum(powers, axis=0, keepdims=True)
            my_stat[2:3, at] = jnp.sum(jnp.where(hits(i + k), logits, 0.0), axis=0, keepdims=True)

    for dz in range(na):
        for dy in range(1, nb):
            if dz:
                for h in range(steps):
                    take_q(dz, dy, h)
            else:
                take_q(dz, dy)
        first = wrap(zh + (na - dz), na) * nb
        repeat(nb // 2, lambda g: forward(first + g * 2))

    for dz, dy in peers:
        k = dz * nb + dy
        start(my_stat, my_stat, ss_send.at[k], ss_recv.at[k], peer(dz, dy))
    for dz, dy in peers:
        k = dz * nb + dy
        arrive(
            stat.at[member((na - dz) % na, (nb - dy) % nb)], ss_send.at[k], ss_recv.at[k]
        )

    top = stat[0, 0:1, :]
    for i in range(1, nr):
        top = jnp.maximum(top, stat[i, 0:1, :])
    summed = jnp.zeros_like(top)
    positive = jnp.zeros_like(top)
    for i in range(nr):
        summed += stat[i, 1:2, :] * jnp.exp(stat[i, 0:1, :] - top)
        positive += stat[i, 2:3, :]
    totals = top + jnp.log(summed)
    stat[nr, 0:1, :] = jnp.exp(my_stat[0:1, :] - totals)

    def make_delta(i):
        part = ebuf[:, span(i)] * stat[nr, 0:1, span(i)]
        dbuf[:, span(i)] = (part - jnp.where(hits(i), 1.0, 0.0)).astype(BF16)

    def query_part(i):
        part = lax.dot_general(
            dbuf[:, span(i, 2)], pbuf[...], (((0,), (0,)), ((), ())), preferred_element_type=F32
        )
        for k in range(2):
            qpart[i + k] = (part[k * LANES : k * LANES + rows] * inv_temp).astype(BF16)

    def part_at(dz, dy):
        return qpart.at[member(dz, dy)]

    def piece_of(ref, h):
        return ref.at[pl.ds(h * STEP, STEP)]

    for dz in [*range(1, na), 0]:
        first = wrap(zh + dz, na) * nb

        def group(g):
            make_delta(first + g * 2)
            make_delta(first + g * 2 + 1)
            query_part(first + g * 2)

        repeat(nb // 2, group)
        if dz:
            for dy in range(1, nb):
                k = dz * nb + dy
                for h in range(steps):
                    start(
                        piece_of(part_at(dz, dy), h),
                        piece_of(qy_in.at[k], h),
                        gy_send.at[k, h],
                        gy_recv.at[k, h],
                        peer(0, dy),
                    )

    half = count // 2

    def update(core):
        return (
            jnp.dot(
                dbuf[pl.ds(pl.multiple_of(core * half, 16), half), :],
                qbuf[...],
                preferred_element_type=F32,
            )
            * inv_temp
        )

    def block(ref, zl, xx):
        return ref.at[pl.ds(pl.multiple_of((zl * 2 + xx) * rows, 16), rows)]

    psib_out[...] = update(1 - co).astype(BF16)
    order = [(1, 1), (0, 1), (1, 0), (0, 0)]

    def at_order(k):
        dz, dx = order[k]
        return (1 - zl if dz else zl, 1 - xx if dx else xx)

    for k in range(4):
        start(
            block(psib_out, *at_order(k)),
            block(psib_in, *at_order(k)),
            gs_send.at[k],
            gs_recv.at[k],
            sib,
        )
    pacc[...] = update(co)

    for dz in range(1, na):
        for h in range(steps):
            total = piece_of(part_at(dz, 0), h)[...].astype(F32)
            for dy in range(1, nb):
                k = dz * nb + dy
                arrive(piece_of(qy_in.at[k], h), gy_send.at[k, h], gy_recv.at[k, h])
                total += piece_of(qy_in.at[k], h)[...].astype(F32)
            piece_of(qz_out.at[dz], h)[...] = total.astype(BF16)
            start(
                piece_of(qz_out.at[dz], h),
                piece_of(qz_in.at[dz], h),
                gz_send.at[dz, h],
                gz_recv.at[dz, h],
                peer(dz, 0),
            )
    for dy in range(1, nb):
        start(part_at(0, dy), qy_in.at[dy], gy_send.at[dy, 0], gy_recv.at[dy, 0], peer(0, dy))

    def piece(k, h=None):
        mine, came = block(pacc, *at_order(k)), block(psib_in, *at_order(k))
        if h is not None:
            mine, came = piece_of(mine, h), piece_of(came, h)
        return mine[...] + came[...].astype(F32)

    def sib_arrive(k):
        arrive(block(psib_in, *at_order(k)), gs_send.at[k], gs_recv.at[k])

    sib_arrive(0)
    px_out[0] = piece(0).astype(BF16)
    for h in range(steps):
        start(
            piece_of(px_out.at[0], h),
            piece_of(px_in.at[0], h),
            gp_send.at[0, h],
            gp_recv.at[0, h],
            xnb,
        )
    sib_arrive(1)
    px_out[1] = piece(1).astype(BF16)
    start(px_out.at[1], px_in.at[1], gp_send.at[1, 0], gp_recv.at[1, 0], xnb)
    sib_arrive(2)
    for h in range(steps):
        came = piece_of(px_in.at[0], h)
        arrive(came, gp_send.at[0, h], gp_recv.at[0, h])
        out = piece_of(pz_out, h)
        out[...] = (piece(2, h) + came[...].astype(F32)).astype(BF16)
        start(out, piece_of(pz_in, h), gp_send.at[2, h], gp_recv.at[2, h], znb)

    losses = totals - positive
    picked = jnp.zeros((1, LANES), F32)
    for i in range(nr):
        picked = jnp.where(me_r == i, losses[:, i * LANES : (i + 1) * LANES], picked)
    loss_ref[...] = picked[:, :rows]

    grad = part_at(0, 0)[...].astype(F32)
    for dy in range(1, nb):
        arrive(qy_in.at[dy], gy_send.at[dy, 0], gy_recv.at[dy, 0])
        grad += qy_in[dy].astype(F32)
    for dz in range(1, na):
        for h in range(steps):
            arrive(piece_of(qz_in.at[dz], h), gz_send.at[dz, h], gz_recv.at[dz, h])
        grad += qz_in[dz].astype(F32)
    q_unit, q_len = unit_rows(q_ref[...])
    qg_ref[...] = unit_back(q_unit, q_len, grad)
    save_q = pltpu.make_async_copy(qg_ref, qg_hbm, io_sem.at[2])
    save_q.start()

    sib_arrive(3)
    arrive(px_in.at[1], gp_send.at[1, 0], gp_recv.at[1, 0])
    grad = piece(3) + px_in[1].astype(F32)
    for h in range(steps):
        arrive(piece_of(pz_in, h), gp_send.at[2, h], gp_recv.at[2, h])
    grad += pz_in[...].astype(F32)
    p_unit, p_len = unit_rows(p_ref[...])
    pg_ref[...] = unit_back(p_unit, p_len, grad)
    save_p = pltpu.make_async_copy(pg_ref, pg_hbm, io_sem.at[3])
    save_p.start()

    for copy in sent:
        copy.wait_send()
    save_q.wait()
    save_p.wait()


def deliver(a_in, b_in, c_in, a_out, b_out, c_out, sems):
    copies = [
        pltpu.make_async_copy(src, dst, sems.at[k])
        for k, (src, dst) in enumerate([(a_in, a_out), (b_in, b_out), (c_in, c_out)])
    ]
    for copy in copies:
        copy.start()
    for copy in copies:
        copy.wait()


def local(na, nb, queries, passages, positives, inv_temp):
    rows, width = queries.shape
    nr = na * nb
    lanes = nr * LANES
    steps = rows // STEP
    block = (rows, width)
    vmem = pl.BlockSpec(memory_space=pltpu.VMEM)
    smem = pl.BlockSpec(memory_space=pltpu.SMEM)
    anywhere = pl.BlockSpec(memory_space=pl.ANY)
    dma = pltpu.SemaphoreType.DMA
    shapes = (
        jax.ShapeDtypeStruct((1, rows), F32),
        jax.ShapeDtypeStruct(block, BF16),
        jax.ShapeDtypeStruct(block, BF16),
    )
    made = pl.pallas_call(
        functools.partial(kernel, na, nb),
        out_shape=shapes,
        in_specs=[smem, vmem, anywhere, anywhere],
        out_specs=(vmem, anywhere, anywhere),
        scratch_shapes=[
            pltpu.VMEM(block, BF16),
            pltpu.VMEM(block, BF16),
            pltpu.VMEM(block, BF16),
            pltpu.VMEM(block, BF16),
            pltpu.VMEM((lanes, width), BF16),
            pltpu.VMEM((COLS * rows, width), BF16),
            pltpu.VMEM((nr, 8, LANES), jnp.int32),
            pltpu.VMEM((COLS * rows, lanes), F32),
            pltpu.VMEM((COLS * rows, lanes), BF16),
            pltpu.VMEM((nr + 1, 8, lanes), F32),
            pltpu.VMEM((COLS * rows // 2, width), F32),
            pltpu.VMEM((COLS * rows // 2, width), BF16),
            pltpu.VMEM((COLS * rows // 2, width), BF16),
            pltpu.VMEM((2, *block), BF16),
            pltpu.VMEM((2, *block), BF16),
            pltpu.VMEM(block, BF16),
            pltpu.VMEM(block, BF16),
            pltpu.VMEM((nr, *block), BF16),
            pltpu.VMEM((nr, *block), BF16),
            pltpu.VMEM((na, *block), BF16),
            pltpu.VMEM((na, *block), BF16),
            dma((4,)),
            dma((7, steps)),
            dma((7, steps)),
            dma((nr, steps)),
            dma((nr, steps)),
            dma((nr,)),
            dma((nr,)),
            dma((nr,)),
            dma((nr,)),
            dma((4,)),
            dma((4,)),
            dma((3, steps)),
            dma((3, steps)),
            dma((nr, steps)),
            dma((nr, steps)),
            dma((na, steps)),
            dma((na, steps)),
        ],
        compiler_params=pltpu.CompilerParams(
            collective_id=0, has_side_effects=True, vmem_limit_bytes=56 * 1024 * 1024
        ),
    )(inv_temp.reshape(1, 1), positives, queries, passages)
    loss, qg, pg = pl.pallas_call(
        deliver,
        out_shape=shapes,
        in_specs=[anywhere] * 3,
        out_specs=(anywhere,) * 3,
        scratch_shapes=[dma((3,))],
        compiler_params=pltpu.CompilerParams(vmem_limit_bytes=56 * 1024 * 1024),
    )(*made)
    return (loss.reshape(rows), qg, pg)


def solution(mesh):
    na = mesh.shape["pb"] // 4
    nb = mesh.shape["pa"] // 2
    return jax.shard_map(
        functools.partial(local, na, nb),
        mesh=mesh,
        in_specs=(P(("pb", "pa"), None), P(("pb", "pa"), None), P("pb"), P()),
        out_specs=(P(("pb", "pa")), P(("pb", "pa"), None), P(("pb", "pa"), None)),
        check_vma=False,
    )
```

time: 46 us -> 48.5 us (1.054)
  Pallas kernels: 39.6 us -> 47.1 us
  local copies, waits for them, and re-layouts: 4.02 us -> 0 us
  other arithmetic: 0.8 us -> 0 us
    pallas_call x1 -> x2, Pallas kernels: 39.6 us -> 47.1 us  [the longest x1 38.5 us: local(): pl.pallas_call(functools.partial(kernel, na, nb), out_shape=shapes, in_sp...]
    unnamed x7 -> x0, local copies, waits for them, and re-layouts: 3.42 us -> none
    reshape x1 -> x0, other arithmetic: 0.8 us -> none  [local(): code.reshape(1, rows)]
    pad x1 -> x0, local copies, waits for them, and re-layouts: 0.6 us -> none  [local(): jnp.pad(code.reshape(1, rows), ((0, 7), (0, LANES - rows)), constant_valu...]
where the time goes in v2:
time: 48.5 us; the launch traced here: 48.4 us
  Pallas kernels  47.1 us (97%)
  between operations  1.29 us (3%)
    pallas_call x1, Pallas kernels, local(): pl.pallas_call(functools.partial(kernel, na, nb), out_shape=shapes, in_sp...  38.5 us
    pallas_call x1, Pallas kernels, local(): pl.pallas_call(deliver, out_shape=shapes, in_specs=[anywhere] * 3, out_sp...  8.59 us

profile of v2, /device:TPU:0, one launch (start us, length us, event | category | flops | bytes accessed | tf_op | source)
XLA Modules:
  0.0 48.4 jit_solution(5952925445800408254)
XLA Ops:
  1.3 38.5 %shard_map.67 = (f32[1,80]{1,0:T(1,128)}, bf16[80,768]{1,0:T(8,128)(2,1)}, bf16[80,768]{1,0:T(8,128)(2,1)}) custom-call(f32[1,1]{1,0:T(1,128)} %bitcast.2.temp_ref, s32[320]{0:T(512)} %tgt_ref.1, bf16[80,768]{1,0:T(8,128)(2,1)} %q_hbm.1, bf16[80,768]{1,0:T(8,128)(2,1)} %p_hbm.1), custom_call_target="tpu_custom_call" | custom-call | tf_op jit(solution)/shard_map/pallas_call | solution.py:485
  39.8 8.6 %shard_map.68 = (f32[1,80]{1,0:T(1,128)}, bf16[80,768]{1,0:T(8,128)(2,1)}, bf16[80,768]{1,0:T(8,128)(2,1)}) custom-call(f32[1,80]{1,0:T(1,128)} %get-tuple-element.9.a_in, bf16[80,768]{1,0:T(8,128)(2,1)} %get-tuple-element.10.b_in, bf16[80,768]{1,0:T(8,128)(2,1)} %get-tuple-element.11.c_in), custom_call_target="tpu_custom_call" | custom-call | tf_op jit(solution)/shard_map/pallas_call | solution.py:534

commit v3 on v2

--- a/solution.py
+++ b/solution.py
@@ -12,7 +12,6 @@
 BF16 = jnp.bfloat16
 LANES = 128
 COLS = 8
-STEP = 16
 
 
 def unit_rows(values):
@@ -24,6 +23,11 @@
 def unit_back(unit, length, grad):
     along = jnp.sum(unit * grad, axis=1, keepdims=True)
     return ((grad - unit * along) / length).astype(BF16)
+
+
+def cut(rows):
+    first = (rows // 2 + 15) // 16 * 16
+    return [(0, first), (first, rows - first)]
 
 
 def repeat(count, body):
@@ -57,6 +61,7 @@
     ebuf,
     dbuf,
     stat,
+    sidestat,
     pacc,
     psib_out,
     psib_in,
@@ -89,7 +94,8 @@
     rows = q_ref.shape[0]
     width = q_ref.shape[1]
     nr = na * nb
-    steps = rows // STEP
+    pieces = cut(rows)
+    steps = len(pieces)
     pb = lax.axis_index("pb")
     pa = lax.axis_index("pa")
     zh, zl, co = pb // 4, (pb // 2) % 2, pb % 2
@@ -125,13 +131,13 @@
         base = (co * 4 + zl * 2 + xx) * rows
         if h is None:
             return pbuf.at[pl.ds(pl.multiple_of(base, 16), rows)]
-        return pbuf.at[pl.ds(pl.multiple_of(base + h * STEP, 16), STEP)]
+        return pbuf.at[pl.ds(pl.multiple_of(base + pieces[h][0], 16), pieces[h][1])]
 
     def qslot(dz, dy, h=None):
         base = member(dz, dy) * LANES
         if h is None:
             return qbuf.at[pl.ds(pl.multiple_of(base, LANES), rows)]
-        return qbuf.at[pl.ds(pl.multiple_of(base + h * STEP, 16), STEP)]
+        return qbuf.at[pl.ds(pl.multiple_of(base + pieces[h][0], 16), pieces[h][1])]
 
     def tslot(dz, dy):
         return tbuf.at[member(dz, dy)]
@@ -226,61 +232,80 @@
     for dz, dy in peers:
         k = dz * nb + dy
         arrive(tslot((na - dz) % na, (nb - dy) % nb), ts_send.at[k], ts_recv.at[k])
-    take_p(2, 1 - co, zl, xx)
-    take_p(4, 1 - co, 1 - zl, xx)
-    take_p(5, 1 - co, zl, 1 - xx)
-    for h in range(steps):
-        take_p(6, 1 - co, 1 - zl, 1 - xx, h)
 
     inv_temp = temp_ref[0, 0]
     count = COLS * rows
+    half = count // 2
     my_stat = stat.at[me_r]
     down = lax.broadcasted_iota(jnp.int32, (rows, LANES), 0)
-    ids = jnp.concatenate(
-        [
-            down + ((zh * 4 + (j // 2) % 2 * 2 + j // 4) * (nb * 2) + yy * 2 + j % 2) * rows
-            for j in range(COLS)
-        ],
-        axis=0,
-    )
+
+    def ids(core):
+        blocks = [
+            down + ((zh * 4 + (j // 2) * 2 + core) * (nb * 2) + yy * 2 + j % 2) * rows
+            for j in range(COLS // 2)
+        ]
+        return jnp.concatenate(blocks, axis=0)
+
+    own_half = pl.ds(pl.multiple_of(co * half, 16), half)
+    sib_half = pl.ds(pl.multiple_of((1 - co) * half, 16), half)
+    sides = [(0, own_half, ids(co)), (1, sib_half, ids(1 - co))]
 
     def span(i, n=1):
         if isinstance(i, int):
             return pl.ds(i * LANES, n * LANES)
         return pl.ds(pl.multiple_of(i * LANES, LANES), n * LANES)
 
-    def hits(i):
-        return ids == tbuf[i][0:1, :]
-
-    def forward(i):
+    def forward(side, i):
+        k, part, names = sides[side]
         both = (
             lax.dot_general(
-                pbuf[...],
+                pbuf[part, :],
                 qbuf[span(i, 2), :],
                 (((1,), (1,)), ((), ())),
                 preferred_element_type=F32,
             )
             * inv_temp
         )
-        for k in range(2):
-            logits = both[:, k * LANES : (k + 1) * LANES]
+        for g in range(2):
+            logits = both[:, g * LANES : (g + 1) * LANES]
             biggest = jnp.max(logits, axis=0, keepdims=True)
             powers = jnp.exp(logits - biggest)
-            at = span(i + k)
-            ebuf[:, at] = powers
-            my_stat[0:1, at] = biggest
-            my_stat[1:2, at] = jnp.sum(powers, axis=0, keepdims=True)
-            my_stat[2:3, at] = jnp.sum(jnp.where(hits(i + k), logits, 0.0), axis=0, keepdims=True)
-
+            at = span(i + g)
+            ebuf[part, at] = powers
+            hit = names == tbuf[i + g][0:1, :]
+            sidestat[3 * k : 3 * k + 1, at] = biggest
+            sidestat[3 * k + 1 : 3 * k + 2, at] = jnp.sum(powers, axis=0, keepdims=True)
+            sidestat[3 * k + 2 : 3 * k + 3, at] = jnp.sum(
+                jnp.where(hit, logits, 0.0), axis=0, keepdims=True
+            )
+
+    def forward_all(side, dz):
+        first = wrap(zh + (na - dz), na) * nb
+        repeat(nb // 2, lambda g: forward(side, first + g * 2))
+
+    for dy in range(1, nb):
+        take_q(0, dy)
+    forward_all(0, 0)
+    for dz in range(1, na):
+        for dy in range(1, nb):
+            for h in range(steps):
+                take_q(dz, dy, h)
+        forward_all(0, dz)
+    take_p(2, 1 - co, zl, xx)
+    take_p(4, 1 - co, 1 - zl, xx)
+    take_p(5, 1 - co, zl, 1 - xx)
+    for h in range(steps):
+        take_p(6, 1 - co, 1 - zl, 1 - xx, h)
     for dz in range(na):
-        for dy in range(1, nb):
-            if dz:
-                for h in range(steps):
-                    take_q(dz, dy, h)
-            else:
-                take_q(dz, dy)
-        first = wrap(zh + (na - dz), na) * nb
-        repeat(nb // 2, lambda g: forward(first + g * 2))
+        forward_all(1, dz)
+
+    top_own, top_sib = sidestat[0:1, :], sidestat[3:4, :]
+    top_here = jnp.maximum(top_own, top_sib)
+    my_stat[0:1, :] = top_here
+    my_stat[1:2, :] = sidestat[1:2, :] * jnp.exp(top_own - top_here) + sidestat[4:5, :] * jnp.exp(
+        top_sib - top_here
+    )
+    my_stat[2:3, :] = sidestat[2:3, :] + sidestat[5:6, :]
 
     for dz, dy in peers:
         k = dz * nb + dy
@@ -300,11 +325,14 @@
         summed += stat[i, 1:2, :] * jnp.exp(stat[i, 0:1, :] - top)
         positive += stat[i, 2:3, :]
     totals = top + jnp.log(summed)
-    stat[nr, 0:1, :] = jnp.exp(my_stat[0:1, :] - totals)
+    sidestat[6:7, :] = jnp.exp(top_own - totals)
+    sidestat[7:8, :] = jnp.exp(top_sib - totals)
 
     def make_delta(i):
-        part = ebuf[:, span(i)] * stat[nr, 0:1, span(i)]
-        dbuf[:, span(i)] = (part - jnp.where(hits(i), 1.0, 0.0)).astype(BF16)
+        for k, part, names in sides:
+            soft = ebuf[part, span(i)] * sidestat[6 + k : 7 + k, span(i)]
+            hit = names == tbuf[i][0:1, :]
+            dbuf[part, span(i)] = (soft - jnp.where(hit, 1.0, 0.0)).astype(BF16)
 
     def query_part(i):
         part = lax.dot_general(
@@ -317,7 +345,7 @@
         return qpart.at[member(dz, dy)]
 
     def piece_of(ref, h):
-        return ref.at[pl.ds(h * STEP, STEP)]
+        return ref.at[pl.ds(*pieces[h])]
 
     for dz in [*range(1, na), 0]:
         first = wrap(zh + dz, na) * nb
@@ -339,8 +367,6 @@
                         gy_recv.at[k, h],
                         peer(0, dy),
                     )
-
-    half = count // 2
 
     def update(core):
         return (
@@ -456,22 +482,17 @@
     save_p.wait()
 
 
-def deliver(a_in, b_in, c_in, a_out, b_out, c_out, sems):
-    copies = [
-        pltpu.make_async_copy(src, dst, sems.at[k])
-        for k, (src, dst) in enumerate([(a_in, a_out), (b_in, b_out), (c_in, c_out)])
-    ]
-    for copy in copies:
-        copy.start()
-    for copy in copies:
-        copy.wait()
+def deliver(a_in, b_in, c_in, a_out, b_out, c_out):
+    a_out[...] = a_in[...]
+    b_out[...] = b_in[...]
+    c_out[...] = c_in[...]
 
 
 def local(na, nb, queries, passages, positives, inv_temp):
     rows, width = queries.shape
     nr = na * nb
     lanes = nr * LANES
-    steps = rows // STEP
+    steps = len(cut(rows))
     block = (rows, width)
     vmem = pl.BlockSpec(memory_space=pltpu.VMEM)
     smem = pl.BlockSpec(memory_space=pltpu.SMEM)
@@ -497,7 +518,8 @@
             pltpu.VMEM((nr, 8, LANES), jnp.int32),
             pltpu.VMEM((COLS * rows, lanes), F32),
             pltpu.VMEM((COLS * rows, lanes), BF16),
-            pltpu.VMEM((nr + 1, 8, lanes), F32),
+            pltpu.VMEM((nr, 8, lanes), F32),
+            pltpu.VMEM((8, lanes), F32),
             pltpu.VMEM((COLS * rows // 2, width), F32),
             pltpu.VMEM((COLS * rows // 2, width), BF16),
             pltpu.VMEM((COLS * rows // 2, width), BF16),
@@ -534,9 +556,8 @@
     loss, qg, pg = pl.pallas_call(
         deliver,
         out_shape=shapes,
-        in_specs=[anywhere] * 3,
-        out_specs=(anywhere,) * 3,
-        scratch_shapes=[dma((3,))],
+        in_specs=[vmem] * 3,
+        out_specs=(vmem,) * 3,
         compiler_params=pltpu.CompilerParams(vmem_limit_bytes=56 * 1024 * 1024),
     )(*made)
     return (loss.reshape(rows), qg, pg)

time: 48.5 us -> 39.8 us (0.82)
  Pallas kernels: 47.1 us -> 38.3 us
    pallas_call x1, Pallas kernels: 8.59 us -> 1.67 us  [local(): pl.pallas_call(deliver, out_shape=shapes, in_specs=[vmem] * 3, out_specs=...]
    pallas_call x1, Pallas kernels: 38.5 us -> 36.6 us  [local(): pl.pallas_call(functools.partial(kernel, na, nb), out_shape=shapes, in_sp...]
where the time goes in v3:
time: 39.8 us; the launch traced here: 39.6 us
  Pallas kernels  38.3 us (96%)
  between operations  1.29 us (3%)
    pallas_call x1, Pallas kernels, local(): pl.pallas_call(functools.partial(kernel, na, nb), out_shape=shapes, in_sp...  36.6 us
    pallas_call x1, Pallas kernels, local(): pl.pallas_call(deliver, out_shape=shapes, in_specs=[vmem] * 3, out_specs=...  1.67 us

profile of v3, /device:TPU:0, one launch (start us, length us, event | category | flops | bytes accessed | tf_op | source)
XLA Modules:
  0.0 39.6 jit_solution(15632096264378413973)
XLA Ops:
  1.3 36.6 %shard_map.67 = (f32[1,80]{1,0:T(1,128)}, bf16[80,768]{1,0:T(8,128)(2,1)}, bf16[80,768]{1,0:T(8,128)(2,1)}) custom-call(f32[1,1]{1,0:T(1,128)} %bitcast.2.temp_ref, s32[320]{0:T(512)} %tgt_ref.1, bf16[80,768]{1,0:T(8,128)(2,1)} %q_hbm.1, bf16[80,768]{1,0:T(8,128)(2,1)} %p_hbm.1), custom_call_target="tpu_custom_call" | custom-call | tf_op jit(solution)/shard_map/pallas_call | solution.py:506
  37.9 1.7 %shard_map.68 = (f32[1,80]{1,0:T(1,128)}, bf16[80,768]{1,0:T(8,128)(2,1)}, bf16[80,768]{1,0:T(8,128)(2,1)}) custom-call(f32[1,80]{1,0:T(1,128)} %get-tuple-element.9.a_in, bf16[80,768]{1,0:T(8,128)(2,1)} %get-tuple-element.10.b_in, bf16[80,768]{1,0:T(8,128)(2,1)} %get-tuple-element.11.c_in), custom_call_target="tpu_custom_call" | custom-call | tf_op jit(solution)/shard_map/pallas_call | solution.py:556

commit v4 on v3

--- a/solution.py
+++ b/solution.py
@@ -26,8 +26,9 @@
 
 
 def cut(rows):
-    first = (rows // 2 + 15) // 16 * 16
-    return [(0, first), (first, rows - first)]
+    first = 16
+    second = (rows - first) // 2 // 16 * 16
+    return [(0, first), (first, second), (first + second, rows - first - second)]
 
 
 def repeat(count, body):
@@ -128,7 +129,7 @@
         return wrap(zh + dz, na) * nb + wrap(yy + dy, nb)
 
     def pslot(co, zl, xx, h=None):
-        base = (co * 4 + zl * 2 + xx) * rows
+        base = (co * 4 + xx * 2 + zl) * rows
         if h is None:
             return pbuf.at[pl.ds(pl.multiple_of(base, 16), rows)]
         return pbuf.at[pl.ds(pl.multiple_of(base + pieces[h][0], 16), pieces[h][1])]
@@ -241,7 +242,7 @@
 
     def ids(core):
         blocks = [
-            down + ((zh * 4 + (j // 2) * 2 + core) * (nb * 2) + yy * 2 + j % 2) * rows
+            down + ((zh * 4 + (j % 2) * 2 + core) * (nb * 2) + yy * 2 + j // 2) * rows
             for j in range(COLS // 2)
         ]
         return jnp.concatenate(blocks, axis=0)
@@ -368,36 +369,62 @@
                         peer(0, dy),
                     )
 
-    def update(core):
+    def update(core, xx):
+        base = core * half + xx * 2 * rows
         return (
             jnp.dot(
-                dbuf[pl.ds(pl.multiple_of(core * half, 16), half), :],
+                dbuf[pl.ds(pl.multiple_of(base, 16), 2 * rows), :],
                 qbuf[...],
                 preferred_element_type=F32,
             )
             * inv_temp
         )
 
+    def side(ref, xx):
+        return ref.at[pl.ds(pl.multiple_of(xx * 2 * rows, 16), 2 * rows)]
+
     def block(ref, zl, xx):
-        return ref.at[pl.ds(pl.multiple_of((zl * 2 + xx) * rows, 16), rows)]
-
-    psib_out[...] = update(1 - co).astype(BF16)
+        return ref.at[pl.ds(pl.multiple_of((xx * 2 + zl) * rows, 16), rows)]
+
     order = [(1, 1), (0, 1), (1, 0), (0, 0)]
 
     def at_order(k):
         dz, dx = order[k]
         return (1 - zl if dz else zl, 1 - xx if dx else xx)
 
-    for k in range(4):
+    def to_sib(ks):
+        for k in ks:
+            start(
+                block(psib_out, *at_order(k)),
+                block(psib_in, *at_order(k)),
+                gs_send.at[k],
+                gs_recv.at[k],
+                sib,
+            )
+
+    side(psib_out, 1 - xx)[...] = update(1 - co, 1 - xx).astype(BF16)
+    to_sib([0, 1])
+    side(pacc, 1 - xx)[...] = update(co, 1 - xx)
+
+    def piece(k, h=None):
+        mine, came = block(pacc, *at_order(k)), block(psib_in, *at_order(k))
+        if h is not None:
+            mine, came = piece_of(mine, h), piece_of(came, h)
+        return mine[...] + came[...].astype(F32)
+
+    def sib_arrive(k):
+        arrive(block(psib_in, *at_order(k)), gs_send.at[k], gs_recv.at[k])
+
+    sib_arrive(0)
+    px_out[0] = piece(0).astype(BF16)
+    for h in range(steps):
         start(
-            block(psib_out, *at_order(k)),
-            block(psib_in, *at_order(k)),
-            gs_send.at[k],
-            gs_recv.at[k],
-            sib,
-        )
-    pacc[...] = update(co)
-
+            piece_of(px_out.at[0], h),
+            piece_of(px_in.at[0], h),
+            gp_send.at[0, h],
+            gp_recv.at[0, h],
+            xnb,
+        )
     for dz in range(1, na):
         for h in range(steps):
             total = piece_of(part_at(dz, 0), h)[...].astype(F32)
@@ -416,28 +443,11 @@
     for dy in range(1, nb):
         start(part_at(0, dy), qy_in.at[dy], gy_send.at[dy, 0], gy_recv.at[dy, 0], peer(0, dy))
 
-    def piece(k, h=None):
-        mine, came = block(pacc, *at_order(k)), block(psib_in, *at_order(k))
-        if h is not None:
-            mine, came = piece_of(mine, h), piece_of(came, h)
-        return mine[...] + came[...].astype(F32)
-
-    def sib_arrive(k):
-        arrive(block(psib_in, *at_order(k)), gs_send.at[k], gs_recv.at[k])
-
-    sib_arrive(0)
-    px_out[0] = piece(0).astype(BF16)
-    for h in range(steps):
-        start(
-            piece_of(px_out.at[0], h),
-            piece_of(px_in.at[0], h),
-            gp_send.at[0, h],
-            gp_recv.at[0, h],
-            xnb,
-        )
+    side(psib_out, xx)[...] = update(1 - co, xx).astype(BF16)
+    to_sib([2, 3])
+    side(pacc, xx)[...] = update(co, xx)
     sib_arrive(1)
     px_out[1] = piece(1).astype(BF16)
-    start(px_out.at[1], px_in.at[1], gp_send.at[1, 0], gp_recv.at[1, 0], xnb)
     sib_arrive(2)
     for h in range(steps):
         came = piece_of(px_in.at[0], h)
@@ -445,6 +455,8 @@
         out = piece_of(pz_out, h)
         out[...] = (piece(2, h) + came[...].astype(F32)).astype(BF16)
         start(out, piece_of(pz_in, h), gp_send.at[2, h], gp_recv.at[2, h], znb)
+        if h == steps - 2:
+            start(px_out.at[1], px_in.at[1], gp_send.at[1, 0], gp_recv.at[1, 0], xnb)
 
     losses = totals - positive
     picked = jnp.zeros((1, LANES), F32)

time: 39.8 us -> 39.8 us (level)
  no operation moved by 1% of the time
where the time goes in v4:
time: 39.8 us; the launch traced here: 39.7 us
  Pallas kernels  38.4 us (96%)
  between operations  1.29 us (3%)
    pallas_call x1, Pallas kernels, local(): pl.pallas_call(functools.partial(kernel, na, nb), out_shape=shapes, in_sp...  36.7 us
    pallas_call x1, Pallas kernels, local(): pl.pallas_call(deliver, out_shape=shapes, in_specs=[vmem] * 3, out_specs=...  1.67 us

profile of v4, /device:TPU:0, one launch (start us, length us, event | category | flops | bytes accessed | tf_op | source)
XLA Modules:
  0.0 39.7 jit_solution(11706240730523031028)
XLA Ops:
  1.3 36.7 %shard_map.67 = (f32[1,80]{1,0:T(1,128)}, bf16[80,768]{1,0:T(8,128)(2,1)}, bf16[80,768]{1,0:T(8,128)(2,1)}) custom-call(f32[1,1]{1,0:T(1,128)} %bitcast.2.temp_ref, s32[320]{0:T(512)} %tgt_ref.1, bf16[80,768]{1,0:T(8,128)(2,1)} %q_hbm.1, bf16[80,768]{1,0:T(8,128)(2,1)} %p_hbm.1), custom_call_target="tpu_custom_call" | custom-call | tf_op jit(solution)/shard_map/pallas_call | solution.py:518
  38.0 1.7 %shard_map.68 = (f32[1,80]{1,0:T(1,128)}, bf16[80,768]{1,0:T(8,128)(2,1)}, bf16[80,768]{1,0:T(8,128)(2,1)}) custom-call(f32[1,80]{1,0:T(1,128)} %get-tuple-element.9.a_in, bf16[80,768]{1,0:T(8,128)(2,1)} %get-tuple-element.10.b_in, bf16[80,768]{1,0:T(8,128)(2,1)} %get-tuple-element.11.c_in), custom_call_target="tpu_custom_call" | custom-call | tf_op jit(solution)/shard_map/pallas_call | solution.py:568

commit v5 on v4

--- a/solution.py
+++ b/solution.py
@@ -63,6 +63,9 @@
     dbuf,
     stat,
     sidestat,
+    colstat,
+    qsoft,
+    qhit,
     pacc,
     psib_out,
     psib_in,
@@ -311,6 +314,32 @@
     for dz, dy in peers:
         k = dz * nb + dy
         start(my_stat, my_stat, ss_send.at[k], ss_recv.at[k], peer(dz, dy))
+
+    for k, top in enumerate([top_own, top_sib]):
+        colstat[k : k + 1, :] = jnp.exp(top - top_here)
+
+    def query_part(i):
+        parts = jnp.zeros((4 * LANES, width), F32)
+        for k, part, names in sides:
+            softs, picks = [], []
+            for g in range(2):
+                at = span(i + g)
+                hit = names == tbuf[i + g][0:1, :]
+                soft = ebuf[part, at] * colstat[k : k + 1, at]
+                softs.append(jnp.where(hit, 0.0, soft).astype(BF16))
+                picks.append(jnp.where(hit, 1.0, 0.0).astype(BF16))
+            parts += lax.dot_general(
+                jnp.concatenate(softs + picks, axis=1),
+                pbuf[part, :],
+                (((0,), (0,)), ((), ())),
+                preferred_element_type=F32,
+            )
+        for g in range(2):
+            qsoft[i + g] = parts[g * LANES : g * LANES + rows].astype(BF16)
+            qhit[i + g] = parts[(2 + g) * LANES : (2 + g) * LANES + rows].astype(BF16)
+
+    repeat(nr // 2, lambda g: query_part(g * 2))
+
     for dz, dy in peers:
         k = dz * nb + dy
         arrive(
@@ -329,51 +358,53 @@
     sidestat[6:7, :] = jnp.exp(top_own - totals)
     sidestat[7:8, :] = jnp.exp(top_sib - totals)
 
-    def make_delta(i):
-        for k, part, names in sides:
+    colstat[0:1, :] = jnp.exp(top_here - totals)
+    colstat[1:2, :] = jnp.exp(positive - totals) - 1.0
+
+    def query_scale(i):
+        factors = jnp.transpose(colstat[:, span(i)])[:rows]
+        part = qsoft[i].astype(F32) * factors[:, 0:1] + qhit[i].astype(F32) * factors[:, 1:2]
+        qpart[i] = (part * inv_temp).astype(BF16)
+
+    def part_at(dz, dy):
+        return qpart.at[member(dz, dy)]
+
+    def piece_of(ref, h):
+        return ref.at[pl.ds(*pieces[h])]
+
+    for dz in range(1, na):
+        first = wrap(zh + dz, na) * nb
+
+        repeat(nb, lambda g: query_scale(first + g))
+        for dy in range(1, nb):
+            k = dz * nb + dy
+            for h in range(steps):
+                start(
+                    piece_of(part_at(dz, dy), h),
+                    piece_of(qy_in.at[k], h),
+                    gy_send.at[k, h],
+                    gy_recv.at[k, h],
+                    peer(0, dy),
+                )
+
+    def update(k, xx):
+        core = 1 - co if k else co
+        base = core * half + xx * 2 * rows
+        part = pl.ds(pl.multiple_of(base, 16), 2 * rows)
+        names = jnp.concatenate(
+            [down + ((zh * 4 + j * 2 + core) * (nb * 2) + yy * 2 + xx) * rows for j in range(2)],
+            axis=0,
+        )
+
+        def make_delta(i):
             soft = ebuf[part, span(i)] * sidestat[6 + k : 7 + k, span(i)]
             hit = names == tbuf[i][0:1, :]
             dbuf[part, span(i)] = (soft - jnp.where(hit, 1.0, 0.0)).astype(BF16)
 
-    def query_part(i):
-        part = lax.dot_general(
-            dbuf[:, span(i, 2)], pbuf[...], (((0,), (0,)), ((), ())), preferred_element_type=F32
-        )
-        for k in range(2):
-            qpart[i + k] = (part[k * LANES : k * LANES + rows] * inv_temp).astype(BF16)
-
-    def part_at(dz, dy):
-        return qpart.at[member(dz, dy)]
-
-    def piece_of(ref, h):
-        return ref.at[pl.ds(*pieces[h])]
-
-    for dz in [*range(1, na), 0]:
-        first = wrap(zh + dz, na) * nb
-
-        def group(g):
-            make_delta(first + g * 2)
-            make_delta(first + g * 2 + 1)
-            query_part(first + g * 2)
-
-        repeat(nb // 2, group)
-        if dz:
-            for dy in range(1, nb):
-                k = dz * nb + dy
-                for h in range(steps):
-                    start(
-                        piece_of(part_at(dz, dy), h),
-                        piece_of(qy_in.at[k], h),
-                        gy_send.at[k, h],
-                        gy_recv.at[k, h],
-                        peer(0, dy),
-                    )
-
-    def update(core, xx):
-        base = core * half + xx * 2 * rows
+        repeat(nr, make_delta)
         return (
             jnp.dot(
-                dbuf[pl.ds(pl.multiple_of(base, 16), 2 * rows), :],
+                dbuf[part, :],
                 qbuf[...],
                 preferred_element_type=F32,
             )
@@ -402,9 +433,9 @@
                 sib,
             )
 
-    side(psib_out, 1 - xx)[...] = update(1 - co, 1 - xx).astype(BF16)
+    side(psib_out, 1 - xx)[...] = update(1, 1 - xx).astype(BF16)
     to_sib([0, 1])
-    side(pacc, 1 - xx)[...] = update(co, 1 - xx)
+    side(pacc, 1 - xx)[...] = update(0, 1 - xx)
 
     def piece(k, h=None):
         mine, came = block(pacc, *at_order(k)), block(psib_in, *at_order(k))
@@ -440,12 +471,13 @@
                 gz_recv.at[dz, h],
                 peer(dz, 0),
             )
+    repeat(nb, lambda g: query_scale(zh * nb + g))
     for dy in range(1, nb):
         start(part_at(0, dy), qy_in.at[dy], gy_send.at[dy, 0], gy_recv.at[dy, 0], peer(0, dy))
 
-    side(psib_out, xx)[...] = update(1 - co, xx).astype(BF16)
+    side(psib_out, xx)[...] = update(1, xx).astype(BF16)
     to_sib([2, 3])
-    side(pacc, xx)[...] = update(co, xx)
+    side(pacc, xx)[...] = update(0, xx)
     sib_arrive(1)
     px_out[1] = piece(1).astype(BF16)
     sib_arrive(2)
@@ -455,7 +487,7 @@
         out = piece_of(pz_out, h)
         out[...] = (piece(2, h) + came[...].astype(F32)).astype(BF16)
         start(out, piece_of(pz_in, h), gp_send.at[2, h], gp_recv.at[2, h], znb)
-        if h == steps - 2:
+        if h == 0:
             start(px_out.at[1], px_in.at[1], gp_send.at[1, 0], gp_recv.at[1, 0], xnb)
 
     losses = totals - positive
@@ -532,6 +564,9 @@
             pltpu.VMEM((COLS * rows, lanes), BF16),
             pltpu.VMEM((nr, 8, lanes), F32),
             pltpu.VMEM((8, lanes), F32),
+            pltpu.VMEM((8, lanes), F32),
+            pltpu.VMEM((nr, *block), BF16),
+            pltpu.VMEM((nr, *block), BF16),
             pltpu.VMEM((COLS * rows // 2, width), F32),
             pltpu.VMEM((COLS * rows // 2, width), BF16),
             pltpu.VMEM((COLS * rows // 2, width), BF16),

time: 39.8 us -> 38.3 us (0.962)
  Pallas kernels: 38.4 us -> 36.8 us
    pallas_call x1, Pallas kernels: 36.7 us -> 35.2 us  [local(): pl.pallas_call(functools.partial(kernel, na, nb), out_shape=shapes, in_sp...]
where the time goes in v5:
time: 38.3 us; the launch traced here: 38.1 us
  Pallas kernels  36.8 us (96%)
  between operations  1.29 us (3%)
    pallas_call x1, Pallas kernels, local(): pl.pallas_call(functools.partial(kernel, na, nb), out_shape=shapes, in_sp...  35.2 us
    pallas_call x1, Pallas kernels, local(): pl.pallas_call(deliver, out_shape=shapes, in_specs=[vmem] * 3, out_specs=...  1.67 us

profile of v5, /device:TPU:0, one launch (start us, length us, event | category | flops | bytes accessed | tf_op | source)
XLA Modules:
  0.0 38.1 jit_solution(17574516218646923754)
XLA Ops:
  1.3 35.2 %shard_map.67 = (f32[1,80]{1,0:T(1,128)}, bf16[80,768]{1,0:T(8,128)(2,1)}, bf16[80,768]{1,0:T(8,128)(2,1)}) custom-call(f32[1,1]{1,0:T(1,128)} %bitcast.2.temp_ref, s32[320]{0:T(512)} %tgt_ref.1, bf16[80,768]{1,0:T(8,128)(2,1)} %q_hbm.1, bf16[80,768]{1,0:T(8,128)(2,1)} %p_hbm.1), custom_call_target="tpu_custom_call" | custom-call | tf_op jit(solution)/shard_map/pallas_call | solution.py:550
  36.4 1.7 %shard_map.68 = (f32[1,80]{1,0:T(1,128)}, bf16[80,768]{1,0:T(8,128)(2,1)}, bf16[80,768]{1,0:T(8,128)(2,1)}) custom-call(f32[1,80]{1,0:T(1,128)} %get-tuple-element.9.a_in, bf16[80,768]{1,0:T(8,128)(2,1)} %get-tuple-element.10.b_in, bf16[80,768]{1,0:T(8,128)(2,1)} %get-tuple-element.11.c_in), custom_call_target="tpu_custom_call" | custom-call | tf_op jit(solution)/shard_map/pallas_call | solution.py:603

commit v6 on v5

--- a/solution.py
+++ b/solution.py
@@ -131,8 +131,8 @@
     def member(dz, dy):
         return wrap(zh + dz, na) * nb + wrap(yy + dy, nb)
 
-    def pslot(co, zl, xx, h=None):
-        base = (co * 4 + xx * 2 + zl) * rows
+    def pslot(far, zl, xx, h=None):
+        base = (far * 4 + xx * 2 + zl) * rows
         if h is None:
             return pbuf.at[pl.ds(pl.multiple_of(base, 16), rows)]
         return pbuf.at[pl.ds(pl.multiple_of(base + pieces[h][0], 16), pieces[h][1])]
@@ -187,17 +187,18 @@
     qslot(0, 0)[...] = q_unit.astype(BF16)
     load_p.wait()
     p_unit, _ = unit_rows(p_ref[...])
-    pslot(co, zl, xx)[...] = p_unit.astype(BF16)
+    pslot(0, zl, xx)[...] = p_unit.astype(BF16)
     pl.semaphore_wait(barrier, 3 + len(peers))
 
-    def send_p(k, co, zl, xx, to, h=None):
-        slot = pslot(co, zl, xx, h)
+    def send_p(k, zl, xx, to, h=None):
+        far = 1 if k in (2, 4, 5, 6) else 0
         at = (k, h or 0)
-        start(slot, slot, ps_send.at[at], ps_recv.at[at], to)
-
-    def take_p(k, co, zl, xx, h=None):
+        start(pslot(0, zl, xx, h), pslot(far, zl, xx, h), ps_send.at[at], ps_recv.at[at], to)
+
+    def take_p(k, zl, xx, h=None):
+        far = 1 if k in (2, 4, 5, 6) else 0
         at = (k, h or 0)
-        arrive(pslot(co, zl, xx, h), ps_send.at[at], ps_recv.at[at])
+        arrive(pslot(far, zl, xx, h), ps_send.at[at], ps_recv.at[at])
 
     def send_q(dz, dy, slot, to, h=None):
         at = (dz * nb + dy, h or 0)
@@ -211,28 +212,28 @@
     for h in range(steps):
         for dz in range(1, na):
             send_q(dz, 0, qslot(0, 0, h), peer(dz, 0), h)
-        send_p(0, co, zl, xx, znb, h)
+        send_p(0, zl, xx, znb, h)
     for dy in range(1, nb):
         send_q(0, dy, qslot(0, 0), peer(0, dy))
-    send_p(1, co, zl, xx, xnb)
-    send_p(2, co, zl, xx, sib)
+    send_p(1, zl, xx, xnb)
+    send_p(2, zl, xx, sib)
     for dz, dy in peers:
         k = dz * nb + dy
         start(tslot(0, 0), tslot(0, 0), ts_send.at[k], ts_recv.at[k], peer(dz, dy))
 
     for h in range(steps):
-        take_p(0, co, 1 - zl, xx, h)
-        send_p(3, co, 1 - zl, xx, xnb, h)
+        take_p(0, 1 - zl, xx, h)
+        send_p(3, 1 - zl, xx, xnb, h)
         for dz in range(1, na):
             take_q(dz, 0, h)
             for dy in range(1, nb):
                 send_q(dz, dy, qslot(na - dz, 0, h), peer(0, dy), h)
-    send_p(4, co, 1 - zl, xx, sib)
-    take_p(1, co, zl, 1 - xx)
-    send_p(5, co, zl, 1 - xx, sib)
+    send_p(4, 1 - zl, xx, sib)
+    take_p(1, zl, 1 - xx)
+    send_p(5, zl, 1 - xx, sib)
     for h in range(steps):
-        take_p(3, co, 1 - zl, 1 - xx, h)
-        send_p(6, co, 1 - zl, 1 - xx, sib, h)
+        take_p(3, 1 - zl, 1 - xx, h)
+        send_p(6, 1 - zl, 1 - xx, sib, h)
     for dz, dy in peers:
         k = dz * nb + dy
         arrive(tslot((na - dz) % na, (nb - dy) % nb), ts_send.at[k], ts_recv.at[k])
@@ -250,8 +251,8 @@
         ]
         return jnp.concatenate(blocks, axis=0)
 
-    own_half = pl.ds(pl.multiple_of(co * half, 16), half)
-    sib_half = pl.ds(pl.multiple_of((1 - co) * half, 16), half)
+    own_half = pl.ds(0, half)
+    sib_half = pl.ds(half, half)
     sides = [(0, own_half, ids(co)), (1, sib_half, ids(1 - co))]
 
     def span(i, n=1):
@@ -295,11 +296,11 @@
             for h in range(steps):
                 take_q(dz, dy, h)
         forward_all(0, dz)
-    take_p(2, 1 - co, zl, xx)
-    take_p(4, 1 - co, 1 - zl, xx)
-    take_p(5, 1 - co, zl, 1 - xx)
+    take_p(2, zl, xx)
+    take_p(4, 1 - zl, xx)
+    take_p(5, zl, 1 - xx)
     for h in range(steps):
-        take_p(6, 1 - co, 1 - zl, 1 - xx, h)
+        take_p(6, 1 - zl, 1 - xx, h)
     for dz in range(na):
         forward_all(1, dz)
 
@@ -319,7 +320,7 @@
         colstat[k : k + 1, :] = jnp.exp(top - top_here)
 
     def query_part(i):
-        parts = jnp.zeros((4 * LANES, width), F32)
+        tall = []
         for k, part, names in sides:
             softs, picks = [], []
             for g in range(2):
@@ -328,12 +329,13 @@
                 soft = ebuf[part, at] * colstat[k : k + 1, at]
                 softs.append(jnp.where(hit, 0.0, soft).astype(BF16))
                 picks.append(jnp.where(hit, 1.0, 0.0).astype(BF16))
-            parts += lax.dot_general(
-                jnp.concatenate(softs + picks, axis=1),
-                pbuf[part, :],
-                (((0,), (0,)), ((), ())),
-                preferred_element_type=F32,
-            )
+            tall.append(jnp.concatenate(softs + picks, axis=1))
+        parts = lax.dot_general(
+            jnp.concatenate(tall, axis=0),
+            pbuf[...],
+            (((0,), (0,)), ((), ())),
+            preferred_element_type=F32,
+        )
         for g in range(2):
             qsoft[i + g] = parts[g * LANES : g * LANES + rows].astype(BF16)
             qhit[i + g] = parts[(2 + g) * LANES : (2 + g) * LANES + rows].astype(BF16)
@@ -389,7 +391,7 @@
 
     def update(k, xx):
         core = 1 - co if k else co
-        base = core * half + xx * 2 * rows
+        base = k * half + xx * 2 * rows
         part = pl.ds(pl.multiple_of(base, 16), 2 * rows)
         names = jnp.concatenate(
             [down + ((zh * 4 + j * 2 + core) * (nb * 2) + yy * 2 + xx) * rows for j in range(2)],
@@ -490,6 +492,8 @@
         if h == 0:
             start(px_out.at[1], px_in.at[1], gp_send.at[1, 0], gp_recv.at[1, 0], xnb)
 
+    q_unit, q_len = unit_rows(q_ref[...])
+    p_unit, p_len = unit_rows(p_ref[...])
     losses = totals - positive
     picked = jnp.zeros((1, LANES), F32)
     for i in range(nr):
@@ -504,7 +508,6 @@
         for h in range(steps):
             arrive(piece_of(qz_in.at[dz], h), gz_send.at[dz, h], gz_recv.at[dz, h])
         grad += qz_in[dz].astype(F32)
-    q_unit, q_len = unit_rows(q_ref[...])
     qg_ref[...] = unit_back(q_unit, q_len, grad)
     save_q = pltpu.make_async_copy(qg_ref, qg_hbm, io_sem.at[2])
     save_q.start()
@@ -515,7 +518,6 @@
     for h in range(steps):
         arrive(piece_of(pz_in, h), gp_send.at[2, h], gp_recv.at[2, h])
     grad += pz_in[...].astype(F32)
-    p_unit, p_len = unit_rows(p_ref[...])
     pg_ref[...] = unit_back(p_unit, p_len, grad)
     save_p = pltpu.make_async_copy(pg_ref, pg_hbm, io_sem.at[3])
     save_p.start()

time: 38.3 us -> 38.2 us (level)
  no operation moved by 1% of the time
where the time goes in v6:
time: 38.2 us; the launch traced here: 38 us
  Pallas kernels  36.7 us (96%)
  between operations  1.29 us (3%)
    pallas_call x1, Pallas kernels, local(): pl.pallas_call(functools.partial(kernel, na, nb), out_shape=shapes, in_sp...  35.1 us
    pallas_call x1, Pallas kernels, local(): pl.pallas_call(deliver, out_shape=shapes, in_specs=[vmem] * 3, out_specs=...  1.67 us

profile of v6, /device:TPU:0, one launch (start us, length us, event | category | flops | bytes accessed | tf_op | source)
XLA Modules:
  0.0 38.0 jit_solution(17651343279030351390)
XLA Ops:
  1.3 35.1 %shard_map.67 = (f32[1,80]{1,0:T(1,128)}, bf16[80,768]{1,0:T(8,128)(2,1)}, bf16[80,768]{1,0:T(8,128)(2,1)}) custom-call(f32[1,1]{1,0:T(1,128)} %bitcast.2.temp_ref, s32[320]{0:T(512)} %tgt_ref.1, bf16[80,768]{1,0:T(8,128)(2,1)} %q_hbm.1, bf16[80,768]{1,0:T(8,128)(2,1)} %p_hbm.1), custom_call_target="tpu_custom_call" | custom-call | tf_op jit(solution)/shard_map/pallas_call | solution.py:552
  36.3 1.7 %shard_map.68 = (f32[1,80]{1,0:T(1,128)}, bf16[80,768]{1,0:T(8,128)(2,1)}, bf16[80,768]{1,0:T(8,128)(2,1)}) custom-call(f32[1,80]{1,0:T(1,128)} %get-tuple-element.9.a_in, bf16[80,768]{1,0:T(8,128)(2,1)} %get-tuple-element.10.b_in, bf16[80,768]{1,0:T(8,128)(2,1)} %get-tuple-element.11.c_in), custom_call_target="tpu_custom_call" | custom-call | tf_op jit(solution)/shard_map/pallas_call | solution.py:605

commit v7 on v6

--- a/solution.py
+++ b/solution.py
@@ -210,9 +210,9 @@
         arrive(slot, qs_send.at[at], qs_recv.at[at])
 
     for h in range(steps):
+        send_p(0, zl, xx, znb, h)
         for dz in range(1, na):
             send_q(dz, 0, qslot(0, 0, h), peer(dz, 0), h)
-        send_p(0, zl, xx, znb, h)
     for dy in range(1, nb):
         send_q(0, dy, qslot(0, 0), peer(0, dy))
     send_p(1, zl, xx, xnb)
@@ -221,13 +221,22 @@
         k = dz * nb + dy
         start(tslot(0, 0), tslot(0, 0), ts_send.at[k], ts_recv.at[k], peer(dz, dy))
 
-    for h in range(steps):
+    def pass_p(h):
         take_p(0, 1 - zl, xx, h)
         send_p(3, 1 - zl, xx, xnb, h)
+
+    def pass_q(h):
         for dz in range(1, na):
             take_q(dz, 0, h)
             for dy in range(1, nb):
                 send_q(dz, dy, qslot(na - dz, 0, h), peer(0, dy), h)
+
+    pass_p(0)
+    pass_q(0)
+    for h in range(1, steps):
+        pass_p(h)
+    for h in range(1, steps):
+        pass_q(h)
     send_p(4, 1 - zl, xx, sib)
     take_p(1, zl, 1 - xx)
     send_p(5, zl, 1 - xx, sib)
@@ -438,6 +447,8 @@
     side(psib_out, 1 - xx)[...] = update(1, 1 - xx).astype(BF16)
     to_sib([0, 1])
     side(pacc, 1 - xx)[...] = update(0, 1 - xx)
+    side(psib_out, xx)[...] = update(1, xx).astype(BF16)
+    to_sib([2, 3])
 
     def piece(k, h=None):
         mine, came = block(pacc, *at_order(k)), block(psib_in, *at_order(k))
@@ -477,8 +488,6 @@
     for dy in range(1, nb):
         start(part_at(0, dy), qy_in.at[dy], gy_send.at[dy, 0], gy_recv.at[dy, 0], peer(0, dy))
 
-    side(psib_out, xx)[...] = update(1, xx).astype(BF16)
-    to_sib([2, 3])
     side(pacc, xx)[...] = update(0, xx)
     sib_arrive(1)
     px_out[1] = piece(1).astype(BF16)

time: 38.2 us -> 38.5 us (level)
  no operation moved by 1% of the time
where the time goes in v7:
time: 38.5 us; the launch traced here: 38.3 us
  Pallas kernels  37 us (96%)
  between operations  1.29 us (3%)
    pallas_call x1, Pallas kernels, local(): pl.pallas_call(functools.partial(kernel, na, nb), out_shape=shapes, in_sp...  35.4 us
    pallas_call x1, Pallas kernels, local(): pl.pallas_call(deliver, out_shape=shapes, in_specs=[vmem] * 3, out_specs=...  1.67 us

profile of v7, /device:TPU:0, one launch (start us, length us, event | category | flops | bytes accessed | tf_op | source)
XLA Modules:
  0.0 38.3 jit_solution(11284989330394908587)
XLA Ops:
  1.3 35.4 %shard_map.67 = (f32[1,80]{1,0:T(1,128)}, bf16[80,768]{1,0:T(8,128)(2,1)}, bf16[80,768]{1,0:T(8,128)(2,1)}) custom-call(f32[1,1]{1,0:T(1,128)} %bitcast.2.temp_ref, s32[320]{0:T(512)} %tgt_ref.1, bf16[80,768]{1,0:T(8,128)(2,1)} %q_hbm.1, bf16[80,768]{1,0:T(8,128)(2,1)} %p_hbm.1), custom_call_target="tpu_custom_call" | custom-call | tf_op jit(solution)/shard_map/pallas_call | solution.py:561
  36.6 1.7 %shard_map.68 = (f32[1,80]{1,0:T(1,128)}, bf16[80,768]{1,0:T(8,128)(2,1)}, bf16[80,768]{1,0:T(8,128)(2,1)}) custom-call(f32[1,80]{1,0:T(1,128)} %get-tuple-element.9.a_in, bf16[80,768]{1,0:T(8,128)(2,1)} %get-tuple-element.10.b_in, bf16[80,768]{1,0:T(8,128)(2,1)} %get-tuple-element.11.c_in), custom_call_target="tpu_custom_call" | custom-call | tf_op jit(solution)/shard_map/pallas_call | solution.py:614
